TPU v7x, 128 devices: a whole 4x4x4 slice. The times are simulated.
128 devices in a mesh: exp: 16 (over z_lo, y, core), fsdp: 8 (over z_hi, x).
Axes of the slice: x: 4, y: 4, z: 4 (z_hi: 2, z_lo: 2; z = z_hi * 2 + z_lo), core: 2. Of those that a mesh axis runs over, the one named last changes fastest.
Arguments:
- tokens: bfloat16 [512, 7168], P(('exp', 'fsdp')), may hold values from -6 to 6
- expert_ids: int32 [512, 8], P(('exp', 'fsdp')), may hold values from 0 to 31, all different within a row; in each aligned block of 4 rows (0 to 3, 4 to 7, ...) at most 2 rows name the same one
- combine_weight: float32 [512, 8], P(('exp', 'fsdp')), may hold values from 0.1 to 1
- gate_weight: bfloat16 [32, 7168, 2048], P('exp', 'fsdp'), may hold values from -0.0625 to 0.0625
- up_weight: bfloat16 [32, 7168, 2048], P('exp', 'fsdp'), may hold values from -0.0625 to 0.0625
- down_weight: bfloat16 [32, 7168, 2048], P('exp', 'fsdp'), may hold values from -0.125 to 0.125
Outputs:
- mixed: bfloat16 [512, 7168], P(('exp', 'fsdp'))
Inputs may be any that keep to these rules, and one draw needn't show every extreme that they name: `expert_ids`: each row names 8 different experts. Among the 4 rows of one device no expert is named more than 2 times, a bound that some block reaches.
All inputs are finite; a program needn't handle non-finite values.
Results may differ from a plain program's by a relative error of at most 0.025.
Values may be sent and summed in bfloat16 or wider, within the bound.
No kernel may reach another device: no remote copies, remote signals or barrier semaphores. Data moves between devices by JAX's collectives and lax.ppermute only.
A program may use at most 192 MiB of HBM per device.

v0:
```python
import jax
import jax.numpy as jnp
from jax import lax
from jax.sharding import PartitionSpec as P

ROUTE_SCALE = 2.827


def expert_terms(routed, gate_local, up_local, down_local):
    lead_shape = routed.shape[:2]
    outputs = []
    for local_index in range(routed.shape[2]):
        row_block = routed[:, :, local_index].reshape(-1, routed.shape[-1])
        gate_proj = jnp.dot(row_block, gate_local[local_index], preferred_element_type=jnp.float32)
        up_proj = jnp.dot(row_block, up_local[local_index], preferred_element_type=jnp.float32)
        hidden = (jax.nn.silu(gate_proj) * up_proj).astype(jnp.bfloat16)
        partial_out = lax.dot_general(
            hidden,
            down_local[local_index],
            (((1,), (1,)), ((), ())),
            preferred_element_type=jnp.float32,
        )
        outputs.append(partial_out.reshape(lead_shape + (routed.shape[3], routed.shape[4])))
    return jnp.stack(outputs, axis=2)


def on_device(tokens, expert_ids, combine_weight, gate_weight, up_weight, down_weight):
    exp_count = lax.axis_size("exp")
    fsdp_count = lax.axis_size("fsdp")
    rows_dev = tokens.shape[0]
    top_count = expert_ids.shape[1]
    local_experts = gate_weight.shape[0]
    experts = local_experts * exp_count
    capacity = max(2, rows_dev * top_count * 3 // (2 * experts))
    width = tokens.shape[1]
    expert_iota = jnp.arange(experts, dtype=jnp.int32)
    picked = (expert_ids[:, :, None] == expert_iota[None, None, :]).astype(jnp.int32)
    row_hits = jnp.sum(picked, axis=1)
    slot_index = jnp.cumsum(row_hits, axis=0) - row_hits
    slot_iota = jnp.arange(capacity, dtype=jnp.int32)
    placing = row_hits[:, :, None] * (slot_index[:, :, None] == slot_iota[None, None, :]).astype(
        jnp.int32
    )
    outgoing = jnp.einsum(
        "rec,rd->ecd", placing.astype(jnp.bfloat16), tokens, preferred_element_type=jnp.float32
    ).astype(jnp.bfloat16)
    outgoing = outgoing.reshape(exp_count, local_experts, capacity, width)
    inner_shape = (local_experts, capacity, width)
    gate_local, up_local, down_local = (
        lax.all_to_all(gate_weight, "fsdp", split_axis=2, concat_axis=1, tiled=True),
        lax.all_to_all(up_weight, "fsdp", split_axis=2, concat_axis=1, tiled=True),
        lax.all_to_all(down_weight, "fsdp", split_axis=2, concat_axis=1, tiled=True),
    )
    spread = jnp.broadcast_to(outgoing[:, None], (exp_count, fsdp_count) + inner_shape)
    spread = spread.reshape((exp_count * fsdp_count,) + inner_shape)
    arrived = lax.all_to_all(spread, ("exp", "fsdp"), split_axis=0, concat_axis=0, tiled=True)
    partial_terms = expert_terms(
        arrived.reshape((exp_count, fsdp_count) + inner_shape), gate_local, up_local, down_local
    )
    rounded = partial_terms.astype(jnp.bfloat16).reshape((exp_count * fsdp_count,) + inner_shape)
    home_terms = lax.all_to_all(rounded, ("exp", "fsdp"), split_axis=0, concat_axis=0, tiled=True)
    home_terms = home_terms.reshape((exp_count, fsdp_count) + inner_shape)
    expert_out = jnp.sum(home_terms.astype(jnp.float32), axis=1).astype(jnp.bfloat16)
    route_gate = ROUTE_SCALE * combine_weight / jnp.sum(combine_weight, axis=1, keepdims=True)
    row_share = jnp.sum(route_gate[:, :, None] * picked.astype(jnp.float32), axis=1)
    mix_table = row_share[:, :, None] * placing.astype(jnp.float32)
    values = expert_out.reshape(experts, capacity, width).astype(jnp.float32)
    mixed = jnp.einsum("rec,ecd->rd", mix_table, values, precision=lax.Precision.HIGHEST)
    return mixed.astype(jnp.bfloat16)


def solution(mesh):
    return jax.shard_map(
        on_device,
        mesh=mesh,
        in_specs=(
            P(("exp", "fsdp"), None),
            P(("exp", "fsdp"), None),
            P(("exp", "fsdp"), None),
            P("exp", "fsdp", None),
            P("exp", "fsdp", None),
            P("exp", "fsdp", None),
        ),
        out_specs=P(("exp", "fsdp"), None),
        check_vma=False,
    )
```

profile of v0, /device:TPU:1, one launch (start us, length us, event | category | flops | bytes accessed | tf_op | source)
XLA Modules:
  0.0 651.3 jit_solution(8374242957764575462)
XLA Ops:
  0.0 18.9 %copy.58 = bf16[2,896,2048]{1,0,2:T(2,128)(2,1)} copy(bf16[2,896,2048]{2,1,0:T(8,128)(2,1)} %param.9) | data formatting | bytes 14680064 | tf_op args[3]
  18.9 8.2 %all-to-all-start.1 = ((bf16[2,896,2048]{1,0,2:T(2,128)(2,1)}), bf16[2,896,2048]{1,0,2:T(2,128)(2,1)}, u32[]{:S(2)}, u32[]{:S(2)}) async-start(bf16[2,896,2048]{1,0,2:T(2,128)(2,1)} %copy.58), calls=%async_computation.1 | async-start | bytes 14680064 | tf_op jit(solution)/shard_map/all_to_all | solution.py:50
  27.0 18.8 %copy.61 = bf16[2,896,2048]{1,0,2:T(2,128)(2,1)} copy(bf16[2,896,2048]{2,1,0:T(8,128)(2,1)} %param.10) | data formatting | bytes 14680064 | tf_op args[4]
  45.9 66.0 %all-to-all-done.1 = bf16[2,896,2048]{1,0,2:T(2,128)(2,1)} async-done(((bf16[2,896,2048]{1,0,2:T(2,128)(2,1)}), bf16[2,896,2048]{1,0,2:T(2,128)(2,1)}, u32[]{:S(2)}, u32[]{:S(2)}) %all-to-all-start.1) | async-done | bytes 7340064 | tf_op jit(solution)/shard_map/all_to_all | solution.py:50
  111.9 29.1 %all-to-all-start.2 = ((bf16[2,896,2048]{1,0,2:T(2,128)(2,1)}), bf16[2,896,2048]{1,0,2:T(2,128)(2,1)}, u32[]{:S(2)}, u32[]{:S(2)}) async-start(bf16[2,896,2048]{1,0,2:T(2,128)(2,1)} %copy.61), calls=%async_computation.2 | async-start | bytes 14680064 | tf_op jit(solution)/shard_map/all_to_all | solution.py:51
  141.0 18.9 %copy.64 = bf16[2,896,2048]{1,0,2:T(2,128)(2,1)} copy(bf16[2,896,2048]{2,1,0:T(8,128)(2,1)} %param.11) | data formatting | bytes 14680064 | tf_op args[5]
  159.9 65.9 %all-to-all-done.2 = bf16[2,896,2048]{1,0,2:T(2,128)(2,1)} async-done(((bf16[2,896,2048]{1,0,2:T(2,128)(2,1)}), bf16[2,896,2048]{1,0,2:T(2,128)(2,1)}, u32[]{:S(2)}, u32[]{:S(2)}) %all-to-all-start.2) | async-done | bytes 7340064 | tf_op jit(solution)/shard_map/all_to_all | solution.py:51
  225.8 25.9 %all-to-all-start.3 = ((bf16[2,896,2048]{1,0,2:T(2,128)(2,1)}), bf16[2,896,2048]{1,0,2:T(2,128)(2,1)}, u32[]{:S(2)}, u32[]{:S(2)}) async-start(bf16[2,896,2048]{1,0,2:T(2,128)(2,1)} %copy.64), calls=%async_computation.3 | async-start | bytes 14680064 | tf_op jit(solution)/shard_map/all_to_all | solution.py:52
  253.3 83.3 %all-to-all-done.3 = bf16[2,896,2048]{1,0,2:T(2,128)(2,1)} async-done(((bf16[2,896,2048]{1,0,2:T(2,128)(2,1)}), bf16[2,896,2048]{1,0,2:T(2,128)(2,1)}, u32[]{:S(2)}, u32[]{:S(2)}) %all-to-all-start.3) | async-done | bytes 7340064 | tf_op jit(solution)/shard_map/all_to_all | solution.py:52
  336.6 5.5 broadcast_in_dim.5
  342.1 28.8 %all-to-all-start = ((bf16[128,2,2,7168]{3,2,1,0:T(2,128)(2,1)}), bf16[128,2,2,7168]{3,2,1,0:T(2,128)(2,1)}, u32[]{:S(2)}, u32[]{:S(2)}) async-start(bf16[128,2,2,7168]{3,2,1,0:T(2,128)(2,1)} %bitcast.48), calls=%async_computation | async-start | bytes 14680064 | tf_op jit(solution)/shard_map/all_to_all | solution.py:56
  370.9 4.0 copy.59
  374.9 3.7 fusion.22
  378.6 6.3 copy.60
  384.9 6.3 copy.67
  391.2 4.0 copy.62
  395.2 3.8 fusion.23
  398.9 6.3 copy.63
  405.2 6.3 copy.68
  411.5 18.6 %copy.65 = bf16[2,896,8,256]{3,1,2,0:T(8,128)(2,1)} copy(bf16[2,896,8,256]{1,0,3,2:T(2,128)(2,1)} %bitcast.10) | data formatting | bytes 14680064 | tf_op jit(solution)/shard_map/all_to_all | solution.py:52
  430.1 6.7 %fusion.25 = (bf16[1,8,896,256]{3,2,1,0:T(8,128)(2,1)}, bf16[1,8,896,256]{3,2,1,0:T(8,128)(2,1)}) fusion(bf16[2,8,896,256]{3,2,1,0:T(8,128)(2,1)} %bitcast.47), kind=kLoop, calls=%fused_computation.39 | loop fusion | bytes 14680064 | tf_op jit(solution)/shard_map/slice | solution.py:19
  436.8 24.9 %all-to-all-done = bf16[128,2,2,7168]{3,2,1,0:T(2,128)(2,1)} async-done(((bf16[128,2,2,7168]{3,2,1,0:T(2,128)(2,1)}), bf16[128,2,2,7168]{3,2,1,0:T(2,128)(2,1)}, u32[]{:S(2)}, u32[]{:S(2)}) %all-to-all-start) | async-done | bytes 7340064 | tf_op jit(solution)/shard_map/all_to_all | solution.py:56
  461.8 11.1 %fusion.24 = (bf16[16,8,1,2,7168]{4,3,2,1,0:T(2,128)(2,1)}, bf16[16,8,1,2,7168]{4,3,2,1,0:T(2,128)(2,1)}) fusion(bf16[16,8,2,2,7168]{4,3,2,1,0:T(2,128)(2,1)} %bitcast.3), kind=kLoop, calls=%fused_computation.38 | loop fusion | bytes 14680064 | tf_op jit(solution)/shard_map/slice | solution.py:13
  472.9 8.4 %reshape_squeeze.6 = bf16[256,7168]{1,0:T(8,128)(2,1)} reshape(bf16[16,8,1,2,7168]{4,3,2,1,0:T(2,128)(2,1)} %get-tuple-element.9) | data formatting | bytes 7340032 | tf_op jit(solution)/shard_map/reshape;squeeze | solution.py:13
  481.3 8.4 %reshape_squeeze.7 = bf16[256,7168]{1,0:T(8,128)(2,1)} reshape(bf16[16,8,1,2,7168]{4,3,2,1,0:T(2,128)(2,1)} %get-tuple-element.10) | data formatting | bytes 7340032 | tf_op jit(solution)/shard_map/reshape;squeeze | solution.py:13
  489.6 4.4 fusion.26
  496.1 4.4 fusion.27
  502.6 3.3 fusion
  511.6 28.1 %copy.70 = bf16[128,2,2,7168]{3,2,1,0:T(2,128)(2,1)} copy(bf16[128,2,2,7168]{3,0,2,1:T(8,128)(2,1)S(1)} %pad_maximum_fusion) | data formatting | bytes 14680064 | tf_op jit(solution)/shard_map/stack | solution.py:24
  539.7 10.7 %all-to-all-start.4 = ((bf16[128,2,2,7168]{3,2,1,0:T(2,128)(2,1)}), bf16[128,2,2,7168]{3,2,1,0:T(2,128)(2,1)}, u32[]{:S(2)}, u32[]{:S(2)}) async-start(bf16[128,2,2,7168]{3,2,1,0:T(2,128)(2,1)} %copy.70), calls=%async_computation.4 | async-start | bytes 14680064 | tf_op jit(solution)/shard_map/all_to_all | solution.py:61
  550.7 90.8 %all-to-all-done.4 = bf16[128,2,2,7168]{3,2,1,0:T(2,128)(2,1)} async-done(((bf16[128,2,2,7168]{3,2,1,0:T(2,128)(2,1)}), bf16[128,2,2,7168]{3,2,1,0:T(2,128)(2,1)}, u32[]{:S(2)}, u32[]{:S(2)}) %all-to-all-start.4) | async-done | bytes 7340064 | tf_op jit(solution)/shard_map/all_to_all | solution.py:61
  641.5 8.5 %bitcast_reduce_fusion = bf16[16,2,2,7168]{3,2,1,0:T(2,128)(2,1)S(1)} fusion(bf16[128,2,2,7168]{3,2,1,0:T(2,128)(2,1)} %all-to-all-done.4), kind=kLoop, calls=%fused_computation.8 | loop fusion | flops 3211264 | bytes 8257536 | tf_op jit(solution)/shard_map/reduce_sum | solution.py:63
  (33 shorter events, 12.8 us)
Async XLA Ops:
  0.0 251.9 %copy-start = (bf16[4,7168]{1,0:T(4,128)(2,1)S(1)}, bf16[4,7168]{1,0:T(4,128)(2,1)}, u32[]{:S(2)}) copy-start(bf16[4,7168]{1,0:T(4,128)(2,1)} %param.6) | copy-start | bytes 172036
  18.9 93.0 %all-to-all-start.1 = ((bf16[2,896,2048]{1,0,2:T(2,128)(2,1)}), bf16[2,896,2048]{1,0,2:T(2,128)(2,1)}, u32[]{:S(2)}, u32[]{:S(2)}) async-start(bf16[2,896,2048]{1,0,2:T(2,128)(2,1)} %copy.58), calls=%async_computation.1 | async-start | bytes 14680064 | tf_op jit(solution)/shard_map/all_to_all | solution.py:50
  111.9 114.0 %all-to-all-start.2 = ((bf16[2,896,2048]{1,0,2:T(2,128)(2,1)}), bf16[2,896,2048]{1,0,2:T(2,128)(2,1)}, u32[]{:S(2)}, u32[]{:S(2)}) async-start(bf16[2,896,2048]{1,0,2:T(2,128)(2,1)} %copy.61), calls=%async_computation.2 | async-start | bytes 14680064 | tf_op jit(solution)/shard_map/all_to_all | solution.py:51
  159.9 91.9 %copy-start.7 = (s32[4,8]{1,0:T(4,128)S(1)}, s32[4,8]{1,0:T(4,128)}, u32[]{:S(2)}) copy-start(s32[4,8]{1,0:T(4,128)} %param.7) | copy-start | bytes 388
  225.8 110.7 %all-to-all-start.3 = ((bf16[2,896,2048]{1,0,2:T(2,128)(2,1)}), bf16[2,896,2048]{1,0,2:T(2,128)(2,1)}, u32[]{:S(2)}, u32[]{:S(2)}) async-start(bf16[2,896,2048]{1,0,2:T(2,128)(2,1)} %copy.64), calls=%async_computation.3 | async-start | bytes 14680064 | tf_op jit(solution)/shard_map/all_to_all | solution.py:52
  342.1 119.7 %all-to-all-start = ((bf16[128,2,2,7168]{3,2,1,0:T(2,128)(2,1)}), bf16[128,2,2,7168]{3,2,1,0:T(2,128)(2,1)}, u32[]{:S(2)}, u32[]{:S(2)}) async-start(bf16[128,2,2,7168]{3,2,1,0:T(2,128)(2,1)} %bitcast.48), calls=%async_computation | async-start | bytes 14680064 | tf_op jit(solution)/shard_map/all_to_all | solution.py:56
  489.6 4.4 copy-start.4
  489.6 5.3 copy-start.6
  496.1 4.4 copy-start.3
  496.1 5.3 copy-start.5
  502.6 3.4 copy-start.2
  539.7 10.7 %copy-start.8 = (f32[4,8]{1,0:T(4,128)S(1)}, f32[4,8]{1,0:T(4,128)}, u32[]{:S(2)}) copy-start(f32[4,8]{1,0:T(4,128)} %param.8) | copy-start | bytes 388
  539.7 101.8 %all-to-all-start.4 = ((bf16[128,2,2,7168]{3,2,1,0:T(2,128)(2,1)}), bf16[128,2,2,7168]{3,2,1,0:T(2,128)(2,1)}, u32[]{:S(2)}, u32[]{:S(2)}) async-start(bf16[128,2,2,7168]{3,2,1,0:T(2,128)(2,1)} %copy.70), calls=%async_computation.4 | async-start | bytes 14680064 | tf_op jit(solution)/shard_map/all_to_all | solution.py:61
  550.6 100.7 %copy-start.1 = (bf16[4,7168]{1,0:T(4,128)(2,1)S(1)}, bf16[4,7168]{1,0:T(4,128)(2,1)}, u32[]{:S(2)}) copy-start(bf16[4,7168]{1,0:T(4,128)(2,1)} %param.6) | copy-start | bytes 172036
where the time goes:
time: 657 us; the launch traced here: 651 us
  waiting for transfers between devices  331 us (50%)
  local copies, waits for them, and re-layouts  187 us (28%)
  starting transfers between devices  103 us (16%)
  matrix products  18.9 us (3%)
  other arithmetic  11.7 us (2%)
    all_to_all x1, waiting for transfers between devices, on_device(): lax.all_to_all(rounded, ('exp', 'fsdp'), split_axis=0, concat_axis=0, til...  90.8 us
    all_to_all x1, waiting for transfers between devices, on_device(): lax.all_to_all(down_weight, 'fsdp', split_axis=2, concat_axis=1, tiled=True)  83.3 us
    all_to_all x1, waiting for transfers between devices, on_device(): lax.all_to_all(gate_weight, 'fsdp', split_axis=2, concat_axis=1, tiled=True)  66 us
    all_to_all x1, waiting for transfers between devices, on_device(): lax.all_to_all(up_weight, 'fsdp', split_axis=2, concat_axis=1, tiled=True)  65.9 us
    unnamed x21, local copies, waits for them, and re-layouts  58.4 us
    all_to_all x1, starting transfers between devices, on_device(): lax.all_to_all(up_weight, 'fsdp', split_axis=2, concat_axis=1, tiled=True)  29.1 us
    all_to_all x1, starting transfers between devices, on_device(): lax.all_to_all(spread, ('exp', 'fsdp'), split_axis=0, concat_axis=0, tile...  28.8 us
    another operation x1, local copies, waits for them, and re-layouts, expert_terms(): return jnp.stack(outputs, axis=2)  28.1 us
  transfers between devices with their start and end apart: 5, of which 5 were waited for; matrix products, arithmetic and copies ran while one was open for 16% of the time, Pallas kernels for 0%

commit v1 on v0

v1 whole, which is shorter than its diff:
```python
import jax
import jax.numpy as jnp
from jax import lax
from jax.experimental import pallas as pl
from jax.experimental.pallas import tpu as pltpu
from jax.sharding import PartitionSpec as P

ROUTE_SCALE = 2.827
META = 128
BOTH = ("exp", "fsdp")


def params(mib):
    return pltpu.CompilerParams(vmem_limit_bytes=mib * 1024 * 1024)


def dot(a, b, dims):
    return lax.dot_general(a, b, (dims, ((), ())), preferred_element_type=jnp.float32)


def pack_rows(tokens, expert_ids, combine_weight, exp_count, fsdp_count, local_experts):
    rows, width = tokens.shape
    experts = exp_count * local_experts
    picked = expert_ids[:, :, None] == jnp.arange(experts, dtype=jnp.int32)[None, None, :]
    route_gate = ROUTE_SCALE * combine_weight / jnp.sum(combine_weight, axis=1, keepdims=True)
    share = jnp.sum(jnp.where(picked, route_gate[:, :, None], 0.0), axis=1)
    hits = jnp.any(picked, axis=1).astype(jnp.int32)
    earlier = jnp.stack([jnp.sum(hits[:row], axis=0) for row in range(rows)])
    code = (hits * (earlier + 1)).astype(jnp.bfloat16)
    high = share.astype(jnp.bfloat16)
    low = (share - high.astype(jnp.float32)).astype(jnp.bfloat16)
    meta = jnp.stack([code, high, low], axis=1).reshape(rows, 3, exp_count, local_experts)
    meta = meta.transpose(2, 0, 1, 3).reshape(exp_count, 1, rows, 3 * local_experts)
    meta = jnp.pad(meta, ((0, 0), (0, 0), (0, 0), (0, META - 3 * local_experts)))
    slices = tokens.reshape(rows, fsdp_count, width // fsdp_count).transpose(1, 0, 2)[None]
    return jnp.concatenate(
        [
            jnp.broadcast_to(slices, (exp_count,) + slices.shape[1:]),
            jnp.broadcast_to(meta, (exp_count, fsdp_count) + meta.shape[2:]),
        ],
        axis=3,
    )


def placing(meta, local, slots, rows_dev):
    rows = meta.shape[0]
    code = meta[:, local : local + 1].astype(jnp.float32).astype(jnp.int32)
    cap = slots * rows_dev // rows
    block = lax.broadcasted_iota(jnp.int32, (rows, 1), 0) // rows_dev
    slot = jnp.where(code > 0, block * cap + code - 1, -1)
    return (slot == lax.broadcasted_iota(jnp.int32, (rows, slots), 1)).astype(jnp.bfloat16)


def project(rows_in, gate_weight, up_weight, slots, rows_dev, fsdp_count, tile):
    experts, depth, units = gate_weight.shape
    rows = rows_in.shape[0]
    part = slots // fsdp_count

    def body(rows_ref, gate_ref, up_ref, out_ref, held):
        local = pl.program_id(0)

        @pl.when(pl.program_id(1) == 0)
        def _():
            meta = rows_ref[:, depth:]
            for index in range(experts):

                @pl.when(local == index)
                def _():
                    place = placing(meta, index, slots, rows_dev)
                    held[...] = dot(place, rows_ref[:, :depth], ((0,), (0,))).astype(jnp.bfloat16)

        for which, ref in enumerate((gate_ref, up_ref)):
            value = dot(held[...], ref[0], ((1,), (0,))).astype(jnp.bfloat16)
            out_ref[:, 0, which] = value.reshape(fsdp_count, part, tile)

    return pl.pallas_call(
        body,
        grid=(experts, units // tile),
        out_shape=jax.ShapeDtypeStruct((fsdp_count, experts, 2, part, units), jnp.bfloat16),
        in_specs=[
            pl.BlockSpec((rows, rows_in.shape[1]), lambda e, n: (0, 0)),
            pl.BlockSpec((1, depth, tile), lambda e, n: (e, 0, n)),
            pl.BlockSpec((1, depth, tile), lambda e, n: (e, 0, n)),
        ],
        out_specs=pl.BlockSpec((fsdp_count, 1, 2, part, tile), lambda e, n: (0, e, 0, 0, n)),
        scratch_shapes=[pltpu.VMEM((slots, depth), jnp.bfloat16)],
        compiler_params=params(40),
        cost_estimate=pl.CostEstimate(
            flops=4 * experts * slots * depth * units,
            bytes_accessed=4 * experts * depth * units + 4 * experts * slots * units,
            transcendentals=0,
        ),
    )(rows_in, gate_weight, up_weight)


def activate(partials, tile):
    fsdp_count, experts, _, part, units = partials.shape

    def body(in_ref, out_ref):
        total = in_ref[0].astype(jnp.float32)
        for source in range(1, fsdp_count):
            total += in_ref[source].astype(jnp.float32)
        gate, up = total[:, 0], total[:, 1]
        hidden = (gate / (1.0 + jnp.exp(-gate)) * up).astype(jnp.bfloat16)
        for target in range(fsdp_count):
            out_ref[target] = hidden

    return pl.pallas_call(
        body,
        grid=(units // tile,),
        out_shape=jax.ShapeDtypeStruct((fsdp_count, experts, part, units), jnp.bfloat16),
        in_specs=[pl.BlockSpec((fsdp_count, experts, 2, part, tile), lambda n: (0, 0, 0, 0, n))],
        out_specs=pl.BlockSpec((fsdp_count, experts, part, tile), lambda n: (0, 0, 0, n)),
        compiler_params=params(40),
    )(partials)


def finish(rows_in, hidden, down_weight, slots, rows_dev, tile):
    fsdp_count, experts, part, units = hidden.shape
    features = down_weight.shape[1]
    rows = rows_in.shape[0]
    steps = units // tile

    def body(meta_ref, hidden_ref, down_ref, out_ref, total, mixed):
        local, step = pl.program_id(0), pl.program_id(1)
        value = dot(hidden_ref[:, 0].reshape(slots, tile), down_ref[0], ((1,), (1,)))

        @pl.when(step == 0)
        def _():
            total[...] = value

        @pl.when(step > 0)
        def _():
            total[...] += value

        for index in range(experts):

            @pl.when((local == index) & (step == steps - 1))
            def _():
                meta = meta_ref[...]
                place = placing(meta, index, slots, rows_dev)
                high = meta[:, experts + index : experts + index + 1].astype(jnp.float32)
                low = meta[:, 2 * experts + index : 2 * experts + index + 1].astype(jnp.float32)
                term = dot(place, total[...].astype(jnp.bfloat16), ((1,), (0,))) * (high + low)
                if index == 0:
                    mixed[...] = term
                else:
                    mixed[...] += term
                if index == experts - 1:
                    out_ref[...] = mixed[...].astype(jnp.bfloat16)

    return pl.pallas_call(
        body,
        grid=(experts, steps),
        out_shape=jax.ShapeDtypeStruct((rows, features), jnp.bfloat16),
        in_specs=[
            pl.BlockSpec((rows, META), lambda e, k: (0, features // META)),
            pl.BlockSpec((fsdp_count, 1, part, tile), lambda e, k: (0, e, 0, k)),
            pl.BlockSpec((1, features, tile), lambda e, k: (e, 0, k)),
        ],
        out_specs=pl.BlockSpec((rows, features), lambda e, k: (0, 0)),
        scratch_shapes=[pltpu.VMEM((slots, features), jnp.float32), pltpu.VMEM((rows, features), jnp.float32)],
        compiler_params=params(40),
        cost_estimate=pl.CostEstimate(
            flops=2 * experts * slots * features * units,
            bytes_accessed=2 * experts * features * units + 2 * experts * slots * units,
            transcendentals=0,
        ),
    )(rows_in, hidden, down_weight)


def on_device(tokens, expert_ids, combine_weight, gate_weight, up_weight, down_weight):
    exp_count, fsdp_count = lax.axis_size("exp"), lax.axis_size("fsdp")
    devices = exp_count * fsdp_count
    rows_dev, width = tokens.shape
    local_experts, depth, units = gate_weight.shape
    experts = exp_count * local_experts
    cap = max(2, rows_dev * expert_ids.shape[1] * 3 // (2 * experts))
    slots = devices * cap
    sent = pack_rows(tokens, expert_ids, combine_weight, exp_count, fsdp_count, local_experts)
    sent = sent.reshape((devices,) + sent.shape[2:])
    rows_in = lax.all_to_all(sent, BOTH, 0, 0, tiled=True).reshape(devices * rows_dev, depth + META)
    partials = project(rows_in, gate_weight, up_weight, slots, rows_dev, fsdp_count, 512)
    partials = lax.all_to_all(partials, "fsdp", 0, 0, tiled=True)
    hidden = activate(partials, 256)
    hidden = lax.all_to_all(hidden, "fsdp", 0, 0, tiled=True)
    mixed = finish(rows_in, hidden, down_weight, slots, rows_dev, 512)
    home = lax.all_to_all(mixed.reshape(devices, rows_dev, depth), BOTH, 0, 0, tiled=True)
    home = home.reshape(exp_count, fsdp_count, rows_dev, depth).astype(jnp.float32)
    return jnp.sum(home, axis=0).astype(jnp.bfloat16).transpose(1, 0, 2).reshape(rows_dev, width)


def solution(mesh):
    return jax.shard_map(
        on_device,
        mesh=mesh,
        in_specs=(
            P(BOTH, None),
            P(BOTH, None),
            P(BOTH, None),
            P("exp", "fsdp", None),
            P("exp", "fsdp", None),
            P("exp", "fsdp", None),
        ),
        out_specs=P(BOTH, None),
        check_vma=False,
    )
```

time: 657 us -> 166 us (0.25)
  waiting for transfers between devices: 331 us -> 0 us
  local copies, waits for them, and re-layouts: 187 us -> 5.76 us
  blocking collectives: 0 us -> 137 us
  starting transfers between devices: 103 us -> 0 us
  matrix products: 18.9 us -> 0 us
  Pallas kernels: 0 us -> 18.1 us
  other arithmetic: 11.7 us -> 4.86 us
    all_to_all x5 -> x0, waiting for transfers between devices: 331 us -> none  [the longest x1 90.8 us: on_device(): lax.all_to_all(rounded, ('exp', 'fsdp'), split_axis=0, concat_axis=0, til...]
    all_to_all x0 -> x4, blocking collectives: none -> 137 us  [the longest x1 56 us: on_device(): partials = lax.all_to_all(partials, 'fsdp', 0, 0, tiled=True)]
    all_to_all x5 -> x0, starting transfers between devices: 103 us -> none  [the longest x1 29.1 us: on_device(): lax.all_to_all(up_weight, 'fsdp', split_axis=2, concat_axis=1, tiled=True)]
    unnamed x21 -> x7, local copies, waits for them, and re-layouts: 58.4 us -> 3.94 us
    slice x8 -> x1, local copies, waits for them, and re-layouts: 50.4 us -> 0.02 us  [pack_rows(): earlier = jnp.stack([jnp.sum(hits[:row], axis=0) for row in range(rows)])]
    another operation x5 -> x7, local copies, waits for them, and re-layouts: 45 us -> 0.51 us  [pack_rows(): earlier = jnp.stack([jnp.sum(hits[:row], axis=0) for row in range(rows)])]
    all_to_all x3 -> x0, local copies, waits for them, and re-layouts: 26.6 us -> none  [the longest x1 18.6 us: on_device(): lax.all_to_all(down_weight, 'fsdp', split_axis=2, concat_axis=1, tiled=True)]
    dot_general x8 -> x0, matrix products: 18.9 us -> none  [the longest x2 8.8 us: expert_terms(): jnp.dot(row_block, gate_local[local_index], preferred_element_type=jnp.fl...]
  transfers between devices with their start and end apart: 5 -> 0, of which waited for: 5 -> 0; matrix products, arithmetic and copies ran while one was open for 16% -> 0% of each run, Pallas kernels for 0% -> 0%
where the time goes in v1:
time: 166 us
  blocking collectives  137 us (83%)
  Pallas kernels  18.1 us (11%)
  local copies, waits for them, and re-layouts  5.76 us (3%)
  other arithmetic  4.86 us (3%)
    all_to_all x1, blocking collectives, on_device(): partials = lax.all_to_all(partials, 'fsdp', 0, 0, tiled=True)  56 us
    all_to_all x1, blocking collectives, on_device(): hidden = lax.all_to_all(hidden, 'fsdp', 0, 0, tiled=True)  30.1 us
    all_to_all x1, blocking collectives, on_device(): lax.all_to_all(sent, BOTH, 0, 0, tiled=True)  29.3 us
    all_to_all x1, blocking collectives, on_device(): lax.all_to_all(mixed.reshape(devices, rows_dev, depth), BOTH, 0, 0, tiled...  21.3 us
    pallas_call x1, Pallas kernels, project(): pl.pallas_call(body, grid=(experts, units // tile), out_shape=jax.ShapeDt...  10.1 us
    pallas_call x1, Pallas kernels, finish(): pl.pallas_call(body, grid=(experts, steps), out_shape=jax.ShapeDtypeStruc...  6.4 us
    unnamed x7, local copies, waits for them, and re-layouts  3.94 us

profile of v1, /device:TPU:1, one launch (start us, length us, event | category | flops | bytes accessed | tf_op | source)
XLA Modules:
  0.0 165.5 jit_solution(15950909465816663317)
XLA Ops:
  0.0 0.8 fusion
  0.8 0.1 reduce_or.12
  0.9 0.8 reduce_sum.56
  1.8 0.8 multiply_divide_fusion
  2.5 0.8 select_reduce_fusion
  3.3 0.1 stack.22
  3.4 0.1 copy.40
  3.4 0.1 stack.23
  3.5 0.1 copy.41
  3.6 0.1 stack.24
  3.7 0.1 copy.42
  3.8 0.1 copy.43
  3.9 0.1 copy.44
  4.0 0.1 copy.45
  4.1 0.8 copy.50
  5.0 0.1 fusion.2
  5.1 0.1 copy.47
  5.3 0.2 broadcast_in_dim.18
  5.5 0.6 pad_maximum_fusion
  6.1 29.3 %all_to_all.20 = bf16[128,4,1024]{2,1,0:T(4,128)(2,1)S(1)} all-to-all(bf16[128,4,1024]{2,1,0:T(4,128)(2,1)S(1)} %bitcast.21), channel_id=1, replica_groups=mesh['exp'=16,'fsdp'=8] {'exp','fsdp'}, dimensions={0} | all-to-all | bytes 2097152 | tf_op jit(solution)/shard_map/all_to_all | solution.py:182
  35.4 0.3 reshape.137.rows_ref.meta_ref
  35.7 0.0 copy-start
  35.7 3.1 %copy-done = bf16[2,896,2048]{2,1,0:T(8,128)(2,1)S(1)} copy-done((bf16[2,896,2048]{2,1,0:T(8,128)(2,1)S(1)}, bf16[2,896,2048]{2,1,0:T(8,128)(2,1)}, u32[]{:S(2)}) %copy-start) | copy-done | bytes 7340056
  38.8 10.1 %shard_map.64 = bf16[8,2,2,32,2048]{4,3,2,1,0:T(8,128)(2,1)S(1)} custom-call(bf16[512,1024]{1,0:T(8,128)(2,1)S(1)} %reshape.137.rows_ref.meta_ref, bf16[2,896,2048]{2,1,0:T(8,128)(2,1)S(1)} %copy-done, bf16[2,896,2048]{2,1,0:T(8,128)(2,1)} %up_ref.1), custom_call_target="tpu_custom_call" | custom-call | flops 3758096384 | bytes 18874368 | tf_op jit(solution)/shard_map/pallas_call | solution.py:76
  48.9 0.0 slice-start
  48.9 56.0 %all_to_all.21.in_ref = bf16[8,2,2,32,2048]{4,3,2,1,0:T(8,128)(2,1)S(1)} all-to-all(bf16[8,2,2,32,2048]{4,3,2,1,0:T(8,128)(2,1)S(1)} %shard_map.64), channel_id=1, replica_groups=mesh['exp'=16,'fsdp'=8] {'fsdp'}, dimensions={0} | all-to-all | bytes 8388608 | tf_op jit(solution)/shard_map/all_to_all | solution.py:184
  104.9 1.6 shard_map.65
  106.5 30.1 %all_to_all.22.hidden_ref = bf16[8,2,32,2048]{3,2,1,0:T(8,128)(2,1)S(1)} all-to-all(bf16[8,2,32,2048]{3,2,1,0:T(8,128)(2,1)S(1)} %shard_map.65), channel_id=1, replica_groups=mesh['exp'=16,'fsdp'=8] {'fsdp'}, dimensions={0} | all-to-all | bytes 4194304 | tf_op jit(solution)/shard_map/all_to_all | solution.py:186
  136.6 6.4 %shard_map.66 = bf16[512,896]{1,0:T(8,128)(2,1)S(1)} custom-call(bf16[512,1024]{1,0:T(8,128)(2,1)S(1)} %reshape.137.rows_ref.meta_ref, bf16[8,2,32,2048]{3,2,1,0:T(8,128)(2,1)S(1)} %all_to_all.22.hidden_ref, bf16[2,896,2048]{2,1,0:T(8,128)(2,1)S(1)} %bitcast.20), custom_call_target="tpu_custom_call" | custom-call | flops 1879048192 | bytes 9437184 | tf_op jit(solution)/shard_map/pallas_call | solution.py:152
  143.0 0.2 reshape.138
  143.3 21.3 %all_to_all.23 = bf16[128,4,896]{2,1,0:T(4,128)(2,1)S(1)} all-to-all(bf16[128,4,896]{2,1,0:T(4,128)(2,1)S(1)} %reshape.138), channel_id=1, replica_groups=mesh['exp'=16,'fsdp'=8] {'exp','fsdp'}, dimensions={0} | all-to-all | bytes 1835008 | tf_op jit(solution)/shard_map/all_to_all | solution.py:188
  164.5 1.0 reduce_sum.59
  (14 shorter events, 0.2 us)
Async XLA Ops:
  35.7 3.1 %copy-start = (bf16[2,896,2048]{2,1,0:T(8,128)(2,1)S(1)}, bf16[2,896,2048]{2,1,0:T(8,128)(2,1)}, u32[]{:S(2)}) copy-start(bf16[2,896,2048]{2,1,0:T(8,128)(2,1)} %gate_ref.1) | copy-start | bytes 22020100
  48.9 87.8 %slice-start = ((s8[7340032]{0:T(1024)(128)(4,1)}), s8[3145728]{0:T(1024)(128)(4,1)S(1)}, s32[]{:S(2)}) async-start(s8[7340032]{0:T(1024)(128)(4,1)} %bitcast.19), calls=%async_computation.4 | async-start | bytes 6291456
  104.9 31.7 %slice-start.1 = ((s8[7340032]{0:T(1024)(128)(4,1)}), s8[4194304]{0:T(1024)(128)(4,1)S(1)}, s32[]{:S(2)}) async-start(s8[7340032]{0:T(1024)(128)(4,1)} %bitcast.19), calls=%async_computation.5 | async-start | bytes 8388608

commit v2 on v0

v2 whole, which is shorter than its diff:
```python
import jax
import jax.numpy as jnp
from jax import lax
from jax.experimental import pallas as pl
from jax.experimental.pallas import tpu as pltpu
from jax.sharding import PartitionSpec as P

ROUTE_SCALE = 2.827
META = 128
UNIT = 128
RING = 4
BOTH = ("exp", "fsdp")


def params(mib):
    return pltpu.CompilerParams(vmem_limit_bytes=mib * 1024 * 1024)


def dot(a, b, dims):
    return lax.dot_general(a, b, (dims, ((), ())), preferred_element_type=jnp.float32)


def pack_rows(tokens, expert_ids, combine_weight, exp_count, fsdp_count, experts):
    rows, width = tokens.shape
    depth = width // fsdp_count

    def body(tokens_ref, ids_ref, weight_ref, out_ref):
        ids, weight = ids_ref[...], weight_ref[...]
        gates = ROUTE_SCALE * weight / jnp.sum(weight, axis=1, keepdims=True)
        column = lax.broadcasted_iota(jnp.int32, (rows, META), 1)
        hits = jnp.zeros((rows, META), jnp.float32)
        high_low = jnp.zeros((rows, META), jnp.float32)
        for k in range(ids.shape[1]):
            named, gate = ids[:, k : k + 1], gates[:, k : k + 1]
            high = gate.astype(jnp.bfloat16).astype(jnp.float32)
            hits = jnp.where(column == named, 1.0, hits)
            high_low = jnp.where(column == named + experts, high, high_low)
            high_low = jnp.where(column == named + 2 * experts, gate - high, high_low)
        meta = jnp.where(column < experts, hits, high_low).astype(jnp.bfloat16)
        for f in range(fsdp_count):
            block = jnp.concatenate([tokens_ref[:, f * depth : (f + 1) * depth], meta], axis=1)
            for e in range(exp_count):
                out_ref[e, f] = block

    return pl.pallas_call(
        body,
        out_shape=jax.ShapeDtypeStruct((exp_count, fsdp_count, rows, depth + META), jnp.bfloat16),
        compiler_params=params(32),
    )(tokens, expert_ids, combine_weight)


def position(target, me):
    across = (target // RING + me // RING) % 2
    along = (target + 2 * RING - me) % RING
    return jnp.where(along < 2, along, 5 - along) * 2 + across


def gather_rows(me, rows_in, experts, total, slots):
    rows, depth = rows_in.shape[0], rows_in.shape[1] - META
    part = UNIT // (2 * RING)

    def body(me_ref, rows_ref, out_ref, info_ref, full_ref):
        meta = rows_ref[:, depth:]
        before = lax.broadcasted_iota(jnp.int32, (rows, rows), 1) < lax.broadcasted_iota(jnp.int32, (rows, rows), 0)
        source = lax.broadcasted_iota(jnp.int32, (META, META), 0)
        target = lax.broadcasted_iota(jnp.int32, (META, META), 1)
        wanted = target // experts * total + me_ref[1] * experts + target % experts
        chosen = ((source == wanted) & (target < 3 * experts)).astype(jnp.bfloat16)
        meta = dot(meta, chosen, ((1,), (0,)))
        rank = dot(before.astype(jnp.bfloat16), meta.astype(jnp.bfloat16), ((1,), (0,)))
        column = lax.broadcasted_iota(jnp.int32, (rows, META), 1)
        info = jnp.zeros((rows, META), jnp.float32)
        for index in range(experts):
            hit = meta[:, index : index + 1]
            slot = jnp.where(hit > 0.5, rank[:, index : index + 1], -1.0)
            gate = meta[:, experts + index : experts + index + 1] + meta[:, 2 * experts + index : 2 * experts + index + 1]
            info = jnp.where(column == index, slot, jnp.where(column == experts + index, gate, info))
            place = slot.astype(jnp.int32) == lax.broadcasted_iota(jnp.int32, (rows, slots), 1)
            value = dot(place.astype(jnp.bfloat16), rows_ref[:, :depth], ((0,), (0,))).astype(jnp.bfloat16)
            for block in range(slots // part):
                first = block * part // UNIT * UNIT + position(block % (2 * RING), me_ref[0]) * part
                out_ref[index, pl.ds(pl.multiple_of(first, part), part)] = value[block * part : (block + 1) * part]
            full_ref[index] = (jnp.sum(hit) > UNIT).astype(jnp.int32)
        info_ref[...] = info

    return pl.pallas_call(
        body,
        out_shape=(
            jax.ShapeDtypeStruct((experts, slots, depth), jnp.bfloat16),
            jax.ShapeDtypeStruct((rows, META), jnp.float32),
            jax.ShapeDtypeStruct((experts,), jnp.int32),
        ),
        out_specs=(
            pl.BlockSpec(memory_space=pltpu.VMEM),
            pl.BlockSpec(memory_space=pltpu.VMEM),
            pl.BlockSpec(memory_space=pltpu.SMEM),
        ),
        in_specs=[pl.BlockSpec(memory_space=pltpu.SMEM), pl.BlockSpec(memory_space=pltpu.VMEM)],
        compiler_params=params(32),
    )(me, rows_in)


def extra_unit(units, experts, local):
    return experts + local if units == 2 * experts else experts


def project(full, packed, weight, units, z_first, tile):
    experts, depth, width = weight.shape
    slots = packed.shape[1]
    part = UNIT // (2 * RING)

    def body(full_ref, packed_ref, weight_ref, *outs):
        column = pl.ds(pl.multiple_of(pl.program_id(0) * tile, tile), tile)
        local = pl.program_id(1)

        def put(unit, value):
            value = value.reshape(2 * RING, part, tile)
            for order in range(RING):
                if z_first:
                    sent, kept = outs
                    kept[order, unit, :, column] = value[2 * order]
                    sent[order, unit, :, column] = value[2 * order + 1]
                else:
                    outs[order][:, unit, :, column] = value[2 * order : 2 * order + 2]

        @pl.when(full_ref[local] == 0)
        def _():
            put(local, dot(packed_ref[local, :UNIT], weight_ref[0], ((1,), (0,))).astype(jnp.bfloat16))

        if units > experts:

            @pl.when(full_ref[local] != 0)
            def _():
                value = dot(packed_ref[local], weight_ref[0], ((1,), (0,))).astype(jnp.bfloat16)
                put(local, value[:UNIT])
                put(extra_unit(units, experts, local), value[UNIT:])

    shapes = [(RING, units, part, width)] * 2 if z_first else [(2, units, part, width)] * RING
    return pl.pallas_call(
        body,
        grid=(width // tile, experts),
        out_shape=tuple(jax.ShapeDtypeStruct(shape, jnp.bfloat16) for shape in shapes),
        in_specs=[
            pl.BlockSpec(memory_space=pltpu.SMEM),
            pl.BlockSpec(memory_space=pltpu.VMEM),
            pl.BlockSpec((1, depth, tile), lambda n, e: (e, 0, n)),
        ],
        out_specs=tuple(pl.BlockSpec(memory_space=pltpu.VMEM) for _ in shapes),
        compiler_params=params(32),
        cost_estimate=pl.CostEstimate(
            flops=2 * units * UNIT * depth * width,
            bytes_accessed=2 * experts * depth * width + 2 * units * UNIT * width,
            transcendentals=0,
        ),
    )(full, packed, weight)


def in_pieces(shape, piece, body):
    units, _, width = shape

    def step(index, carry):
        body(index // (width // piece), pl.ds(pl.multiple_of(index % (width // piece) * piece, piece), piece))
        return carry

    lax.fori_loop(0, units * (width // piece), step, 0)


def whole_call(body, shapes, *operands):
    return pl.pallas_call(
        body,
        out_shape=tuple(jax.ShapeDtypeStruct(shape, kind) for shape, kind in shapes),
        in_specs=[pl.BlockSpec(memory_space=pltpu.VMEM)] * len(operands),
        out_specs=tuple(pl.BlockSpec(memory_space=pltpu.VMEM) for _ in shapes),
        compiler_params=params(32),
    )(*operands)


def wide(value):
    return value.astype(jnp.float32)


def fold(kept, came):
    block = kept.shape[1:]

    def body(kept_ref, came_ref, *outs):
        for order, out_ref in enumerate(outs):

            def piece(unit, column):
                total = wide(kept_ref[order, unit, :, column]) + wide(came_ref[order, unit, :, column])
                out_ref[unit, :, column] = total.astype(jnp.bfloat16)

            in_pieces(block, 512, piece)

    return whole_call(body, [(block, jnp.bfloat16)] * RING, kept, came)


def add_along(*terms):
    block = terms[0].shape[1:]

    def body(*refs):
        for side, out_ref in ((1, refs[-2]), (0, refs[-1])):

            def piece(unit, column):
                total = sum(wide(ref[side, unit, :, column]) for ref in refs[1:-2])
                out_ref[unit, :, column] = (total + wide(refs[0][side, unit, :, column])).astype(out_ref.dtype)

            in_pieces(block, 512, piece)

    return whole_call(body, [(block, jnp.bfloat16), (block, jnp.float32)], *terms)


def activate(stays, came, *terms):
    block = stays.shape

    def body(stays_ref, came_ref, *refs):
        def piece(unit, column):
            gate = stays_ref[unit, :, column] + wide(came_ref[unit, :, column])
            up = sum(wide(ref[unit, :, column]) for ref in refs[1:-1]) + wide(refs[0][unit, :, column])
            refs[-1][unit, :, column] = (gate / (1.0 + jnp.exp(-gate)) * up).astype(jnp.bfloat16)

        in_pieces(block, 512, piece)

    return whole_call(body, [(block, jnp.bfloat16)], stays, came, *terms)[0]


def along(value, step):
    return lax.ppermute(value, "fsdp", [(i, i // RING * RING + (i + step) % RING) for i in range(2 * RING)])


def across(value):
    return lax.ppermute(value, "fsdp", [(i, (i + RING) % (2 * RING)) for i in range(2 * RING)])


def to_others(kept, right, left, far):
    return kept, along(right, 1), along(left, -1), along(far, 2)


def from_others(value):
    return along(value, -1), along(value, 1), along(value, 2)


def finish(full, me, info, parts, down_weight, tile):
    units, part, width = parts[0].shape
    experts, features = down_weight.shape[:2]
    rows = info.shape[0]
    count = len(parts)

    def body(full_ref, me_ref, info_ref, *refs):
        part_refs, (down_ref, out_ref, hidden, total, mixed) = refs[:count], refs[count:]
        local = pl.program_id(0)

        @pl.when(local == 0)
        def _():
            mixed[...] = jnp.zeros_like(mixed)

        def put(slots):
            for index, ref in enumerate(part_refs):
                order, side = index // 2, index % 2
                step = (0, 1, RING - 1, 2)[order]
                target = (me_ref[0] // RING + side) % 2 * RING + (me_ref[0] + step) % RING
                for first in range(0, slots, UNIT):
                    unit = extra_unit(units, experts, local) if first else local
                    hidden[pl.ds(pl.multiple_of(target * part + first, part), part)] = ref[unit]

            def step(index, carry):
                chosen = pl.ds(pl.multiple_of(index * tile, tile), tile)
                value = dot(down_ref[local, chosen], hidden[:slots], ((1,), (1,)))
                total[chosen, :slots] = value.astype(jnp.bfloat16)
                return carry

            lax.fori_loop(0, features // tile, step, 0)
            slot = jnp.where(local == 0, info_ref[:, :1], info_ref[:, 1:2])
            gate = jnp.where(local == 0, info_ref[:, 2:3], info_ref[:, 3:4])
            place = slot.astype(jnp.int32) == lax.broadcasted_iota(jnp.int32, (rows, slots), 1)
            mixed[...] += dot(place.astype(jnp.bfloat16), total[:, :slots], ((1,), (1,))) * gate

        @pl.when(full_ref[local] == 0)
        def _():
            put(UNIT)

        if units > experts:

            @pl.when(full_ref[local] != 0)
            def _():
                put(2 * UNIT)

        @pl.when(local == experts - 1)
        def _():
            out_ref[...] = mixed[...].astype(jnp.bfloat16)

    scalars, whole = pl.BlockSpec(memory_space=pltpu.SMEM), pl.BlockSpec(memory_space=pltpu.VMEM)
    return pl.pallas_call(
        body,
        grid=(experts,),
        out_shape=jax.ShapeDtypeStruct((rows, features), jnp.bfloat16),
        in_specs=[scalars, scalars] + [whole] * (count + 2),
        out_specs=whole,
        scratch_shapes=[
            pltpu.VMEM((2 * UNIT, width), jnp.bfloat16),
            pltpu.VMEM((features, 2 * UNIT), jnp.bfloat16),
            pltpu.VMEM((rows, features), jnp.float32),
        ],
        compiler_params=params(24),
        cost_estimate=pl.CostEstimate(
            flops=2 * units * UNIT * features * width,
            bytes_accessed=2 * experts * features * width + 2 * units * UNIT * width,
            transcendentals=0,
        ),
    )(full, me, info, *parts, down_weight)


def on_device(tokens, expert_ids, combine_weight, gate_weight, up_weight, down_weight):
    exp_count, fsdp_count = lax.axis_size("exp"), lax.axis_size("fsdp")
    devices = exp_count * fsdp_count
    rows_dev, width = tokens.shape
    experts, depth, _ = gate_weight.shape
    sent = pack_rows(tokens, expert_ids, combine_weight, exp_count, fsdp_count, exp_count * experts)
    sent = sent.reshape((devices,) + sent.shape[2:])
    rows_in = lax.all_to_all(sent, BOTH, 0, 0, tiled=True).reshape(devices * rows_dev, depth + META)
    me = jnp.stack([lax.axis_index("fsdp"), lax.axis_index("exp")]).astype(jnp.int32)
    packed, info, full = gather_rows(me, rows_in, experts, exp_count * experts, 2 * UNIT)

    def routed(units, full, packed, info, gate_weight, up_weight, down_weight):
        sent, kept = project(full, packed, up_weight, units, True, 1024)
        packed, sent = lax.optimization_barrier((packed, sent))
        gate_terms = project(full, packed, gate_weight, units, False, 1024)
        came = across(sent)
        sent, stays = add_along(*to_others(*gate_terms))
        up_terms = to_others(*fold(kept, came))
        hidden = activate(stays, across(sent), *up_terms)
        other = across(hidden)
        right, left, far = from_others(hidden)
        right_other, left_other, far_other = from_others(other)
        parts = hidden, other, right, right_other, left, left_other, far, far_other
        return finish(full, me, info, parts, down_weight, 448)

    branches = [lambda *operands, units=units: routed(units, *operands) for units in range(experts, 2 * experts + 1)]
    mixed = lax.switch(jnp.sum(full), branches, full, packed, info, gate_weight, up_weight, down_weight)
    home = lax.all_to_all(mixed.reshape(devices, rows_dev, depth), BOTH, 0, 0, tiled=True)
    home = home.reshape(exp_count, fsdp_count, rows_dev, depth).astype(jnp.float32)
    return jnp.sum(home, axis=0).astype(jnp.bfloat16).transpose(1, 0, 2).reshape(rows_dev, width)


def solution(mesh):
    return jax.shard_map(
        on_device,
        mesh=mesh,
        in_specs=(
            P(BOTH, None),
            P(BOTH, None),
            P(BOTH, None),
            P("exp", "fsdp", None),
            P("exp", "fsdp", None),
            P("exp", "fsdp", None),
        ),
        out_specs=P(BOTH, None),
        check_vma=False,
    )
```

time: 657 us -> 129 us (0.20)
  waiting for transfers between devices: 331 us -> 42.9 us
  local copies, waits for them, and re-layouts: 187 us -> 2.67 us
  starting transfers between devices: 103 us -> 30.5 us
  blocking collectives: 0 us -> 32 us
  matrix products: 18.9 us -> 0 us
  Pallas kernels: 0 us -> 17.9 us
  other arithmetic: 11.7 us -> 1.72 us
    all_to_all x5 -> x1, waiting for transfers between devices: 331 us -> 17.9 us  [on_device(): lax.all_to_all(sent, BOTH, 0, 0, tiled=True)]
    all_to_all x5 -> x1, starting transfers between devices: 103 us -> 11.5 us  [on_device(): lax.all_to_all(sent, BOTH, 0, 0, tiled=True)]
    unnamed x21 -> x6, local copies, waits for them, and re-layouts: 58.4 us -> 2.18 us
    slice x8 -> x0, local copies, waits for them, and re-layouts: 50.4 us -> none  [the longest x3 16.3 us: expert_terms(): up_local[local_index]]
    another operation x5 -> x0, local copies, waits for them, and re-layouts: 45 us -> none  [the longest x1 28.1 us: expert_terms(): return jnp.stack(outputs, axis=2)]
    all_to_all x0 -> x1, blocking collectives: none -> 32 us  [on_device(): lax.all_to_all(mixed.reshape(devices, rows_dev, depth), BOTH, 0, 0, tiled...]
    all_to_all x3 -> x0, local copies, waits for them, and re-layouts: 26.6 us -> none  [the longest x1 18.6 us: on_device(): lax.all_to_all(down_weight, 'fsdp', split_axis=2, concat_axis=1, tiled=True)]
    ppermute x0 -> x15, waiting for transfers between devices: none -> 25 us  [the longest x12 22.1 us: along(): lax.ppermute(value, 'fsdp', [(i, i // RING * RING + (i + step) % RING) fo...]
  transfers between devices with their start and end apart: 5 -> 16, of which waited for: 5 -> 10; matrix products, arithmetic and copies ran while one was open for 16% -> 0% of each run, Pallas kernels for 0% -> 3%
where the time goes in v2:
time: 129 us
  waiting for transfers between devices  42.9 us (33%)
  blocking collectives  32 us (25%)
  starting transfers between devices  30.5 us (24%)
  Pallas kernels  17.9 us (14%)
  local copies, waits for them, and re-layouts  2.67 us (2%)
  other arithmetic  1.72 us (1%)
    all_to_all x1, blocking collectives, on_device(): lax.all_to_all(mixed.reshape(devices, rows_dev, depth), BOTH, 0, 0, tiled...  32 us
    ppermute x12, waiting for transfers between devices, along(): lax.ppermute(value, 'fsdp', [(i, i // RING * RING + (i + step) % RING) fo...  22.1 us
    all_to_all x1, waiting for transfers between devices, on_device(): lax.all_to_all(sent, BOTH, 0, 0, tiled=True)  17.9 us
    ppermute x12, starting transfers between devices, along(): lax.ppermute(value, 'fsdp', [(i, i // RING * RING + (i + step) % RING) fo...  13.3 us
    all_to_all x1, starting transfers between devices, on_device(): lax.all_to_all(sent, BOTH, 0, 0, tiled=True)  11.5 us
    pallas_call x2, Pallas kernels, project(): pl.pallas_call(body, grid=(width // tile, experts), out_shape=tuple((jax....  8.31 us
    ppermute x3, starting transfers between devices, across(): lax.ppermute(value, 'fsdp', [(i, (i + RING) % (2 * RING)) for i in range(...  5.61 us
    pallas_call x1, Pallas kernels, finish(): pl.pallas_call(body, grid=(experts,), out_shape=jax.ShapeDtypeStruct((row...  4.69 us
  transfers between devices with their start and end apart: 16, of which 10 were waited for; matrix products, arithmetic and copies ran while one was open for 0% of the time, Pallas kernels for 3%

profile of v2, /device:TPU:1, one launch (start us, length us, event | category | flops | bytes accessed | tf_op | source)
XLA Modules:
  0.0 128.7 jit_solution(2132884766100964358)
XLA Ops:
  0.0 0.8 copy-done
  0.8 0.7 copy-done.1
  1.5 0.7 copy-done.2
  2.2 1.3 shard_map.64
  3.4 11.5 %all-to-all-start = ((bf16[128,4,1024]{2,1,0:T(4,128)(2,1)}), bf16[128,4,1024]{2,1,0:T(4,128)(2,1)S(1)}, u32[]{:S(2)}, u32[]{:S(2)}) async-start(bf16[128,4,1024]{2,1,0:T(4,128)(2,1)} %bitcast.2), calls=%async_computation | async-start | bytes 2097152 | tf_op jit(solution)/shard_map/all_to_all | solution.py:319
  15.0 17.9 %all-to-all-done = bf16[128,4,1024]{2,1,0:T(4,128)(2,1)S(1)} async-done(((bf16[128,4,1024]{2,1,0:T(4,128)(2,1)}), bf16[128,4,1024]{2,1,0:T(4,128)(2,1)S(1)}, u32[]{:S(2)}, u32[]{:S(2)}) %all-to-all-start) | async-done | bytes 1048608 | tf_op jit(solution)/shard_map/all_to_all | solution.py:319
  33.2 2.5 %shard_map.65 = (bf16[2,256,896]{2,1,0:T(8,128)(2,1)S(1)}, f32[512,128]{1,0:T(8,128)S(1)}, s32[2]{0:T(128)S(1)}) custom-call(s32[2]{0:T(128)S(1)} %pad_add_fusion.me_ref, bf16[512,1024]{1,0:T(8,128)(2,1)S(1)} %reshape.16.rows_ref), custom_call_target="tpu_custom_call" | custom-call | tf_op jit(solution)/shard_map/pallas_call | solution.py:86
  35.8 0.6 reduce_sum.21
  37.0 58.4 %conditional.1 = (bf16[512,896]{1,0:T(8,128)(2,1)S(1)}) conditional(s32[]{:T(128)} %clamp.3, (s32[2]{0:T(128)S(1)}, bf16[2,256,896]{2,1,0:T(8,128)(2,1)S(1)}, bf16[2,896,2048]{2,1,0:T(8,128)(2,1)}, bf16[2,896,2048]{2,1,0:T(8,128)(2,1)}, s32[2]{0:T(128)S(1)}, /*index=5*/f32[512,128]{1,0:T(8,128)S(1)}, ...), branch_computations={%region_1.0_spmd, %region_2.0_spmd, %region_3.0_spmd} | conditional | flops 5637144576 | bytes 101712560 | solution.py:338
  37.1 5.5 %branch_0_fun.6 = (bf16[4,2,16,2048]{3,2,1,0:T(8,128)(2,1)S(1)}, bf16[4,2,16,2048]{3,2,1,0:T(8,128)(2,1)S(1)}) custom-call(s32[2]{0:T(128)S(1)} %get-tuple-element.50.full_ref, bf16[2,256,896]{2,1,0:T(8,128)(2,1)S(1)} %get-tuple-element.57.packed_ref, bf16[2,896,2048]{2,1,0:T(8,128)(2,1)} %get-tuple-element.55.weight_ref), custom_call_target="tpu_custom_call" | custom-call | flops 939524096 | bytes 8388608 | tf_op jit(solution)/shard_map/cond/branch_0_fun/pallas_call | solution.py:139
  42.6 1.9 %collective-permute-start.4 = (bf16[4,2,16,2048]{3,2,1,0:T(8,128)(2,1)S(1)}, bf16[4,2,16,2048]{3,2,1,0:T(8,128)(2,1)S(1)}, u32[]{:S(2)}, u32[]{:S(2)}) collective-permute-start(bf16[4,2,16,2048]{3,2,1,0:T(8,128)(2,1)S(1)} %get-tuple-element.66), channel_id=1, source_target_pairs={{0,4},{1,5},{2,6},{3,7},{4,0},{5,1},{6,2},{7,3},{8,12},{9,13},{10,... | collective-permute-start | bytes 1572872 | tf_op jit(solution)/shard_map/cond/branch_0_fun/ppermute | solution.py:231
  44.5 2.8 %branch_0_fun.7 = (bf16[2,2,16,2048]{3,2,1,0:T(8,128)(2,1)S(1)}, bf16[2,2,16,2048]{3,2,1,0:T(8,128)(2,1)S(1)}, bf16[2,2,16,2048]{3,2,1,0:T(8,128)(2,1)S(1)}, bf16[2,2,16,2048]{3,2,1,0:T(8,128)(2,1)S(1)}) custom-call(s32[2]{0:T(128)S(1)} %get-tuple-element.50.full_ref, bf16[2,256,896]{2,1,0:T(8,128)(2,1)S(1)} %get-tuple-element.57.packed_ref, ...), custom_call_target="tpu_custom_call" | custom-call | flops 939524096 | bytes 8388608 | tf_op jit(solution)/shard_map/cond/branch_0_fun/pallas_call | solution.py:139
  47.7 2.4 %collective-permute-start.1 = (bf16[2,2,16,2048]{3,2,1,0:T(8,128)(2,1)S(1)}, bf16[2,2,16,2048]{3,2,1,0:T(8,128)(2,1)S(1)}, u32[]{:S(2)}, u32[]{:S(2)}) collective-permute-start(bf16[2,2,16,2048]{3,2,1,0:T(8,128)(2,1)S(1)} %get-tuple-element.61), channel_id=1, source_target_pairs={{0,3},{1,0},{2,1},{3,2},{4,7},{5,4},{6,5},{7,6},{8,11},{9,8},{10,9... | collective-permute-start | bytes 786440 | tf_op jit(solution)/shard_map/cond/branch_0_fun/ppermute | solution.py:227
  50.0 0.5 collective-permute-start.2
  50.6 4.3 %collective-permute-done.refs_1_ = bf16[2,2,16,2048]{3,2,1,0:T(8,128)(2,1)S(1)} collective-permute-done((bf16[2,2,16,2048]{3,2,1,0:T(8,128)(2,1)S(1)}, bf16[2,2,16,2048]{3,2,1,0:T(8,128)(2,1)S(1)}, u32[]{:S(2)}, u32[]{:S(2)}) %collective-permute-start) | collective-permute-done | bytes 262176 | tf_op jit(solution)/shard_map/cond/branch_0_fun/ppermute | solution.py:227
  54.9 7.6 %collective-permute-done.2.refs_3_ = bf16[2,2,16,2048]{3,2,1,0:T(8,128)(2,1)S(1)} collective-permute-done((bf16[2,2,16,2048]{3,2,1,0:T(8,128)(2,1)S(1)}, bf16[2,2,16,2048]{3,2,1,0:T(8,128)(2,1)S(1)}, u32[]{:S(2)}, u32[]{:S(2)}) %collective-permute-start.2) | collective-permute-done | bytes 262176 | tf_op jit(solution)/shard_map/cond/branch_0_fun/ppermute | solution.py:227
  62.9 0.5 branch_0_fun.9
  63.7 2.4 %collective-permute-start.6 = (bf16[2,16,2048]{2,1,0:T(8,128)(2,1)S(1)}, bf16[2,16,2048]{2,1,0:T(8,128)(2,1)S(1)}, u32[]{:S(2)}, u32[]{:S(2)}) collective-permute-start(bf16[2,16,2048]{2,1,0:T(8,128)(2,1)S(1)} %get-tuple-element.69), channel_id=1, source_target_pairs={{0,3},{1,0},{2,1},{3,2},{4,7},{5,4},{6,5},{7,6},{8,11},{9,8},{10,9... | collective-permute-start | bytes 393224 | tf_op jit(solution)/shard_map/cond/branch_0_fun/ppermute | solution.py:227
  66.1 2.9 %collective-permute-done.3.came_ref = bf16[2,16,2048]{2,1,0:T(8,128)(2,1)S(1)} collective-permute-done((bf16[2,16,2048]{2,1,0:T(8,128)(2,1)S(1)}, bf16[2,16,2048]{2,1,0:T(8,128)(2,1)S(1)}, u32[]{:S(2)}, u32[]{:S(2)}) %collective-permute-start.3) | collective-permute-done | bytes 131104 | tf_op jit(solution)/shard_map/cond/branch_0_fun/ppermute | solution.py:231
  69.1 0.4 collective-permute-done.6.refs_2_
  69.4 2.9 %collective-permute-done.7.refs_3_ = bf16[2,16,2048]{2,1,0:T(8,128)(2,1)S(1)} collective-permute-done((bf16[2,16,2048]{2,1,0:T(8,128)(2,1)S(1)}, bf16[2,16,2048]{2,1,0:T(8,128)(2,1)S(1)}, u32[]{:S(2)}, u32[]{:S(2)}) %collective-permute-start.7) | collective-permute-done | bytes 131104 | tf_op jit(solution)/shard_map/cond/branch_0_fun/ppermute | solution.py:227
  72.7 3.6 %collective-permute-start.8 = (bf16[2,16,2048]{2,1,0:T(8,128)(2,1)S(1)}, bf16[2,16,2048]{2,1,0:T(8,128)(2,1)S(1)}, u32[]{:S(2)}, u32[]{:S(2)}) collective-permute-start(bf16[2,16,2048]{2,1,0:T(8,128)(2,1)S(1)} %branch_0_fun.10.refs_0_), channel_id=1, source_target_pairs={{0,4},{1,5},{2,6},{3,7},{4,0},{5,1},{6,2},{7,3},{8,12},{9,13},{10,... | collective-permute-start | bytes 393224 | tf_op jit(solution)/shard_map/cond/branch_0_fun/ppermute | solution.py:231
  76.3 2.8 %collective-permute-start.11 = (bf16[2,16,2048]{2,1,0:T(8,128)(2,1)S(1)}, bf16[2,16,2048]{2,1,0:T(8,128)(2,1)S(1)}, u32[]{:S(2)}, u32[]{:S(2)}) collective-permute-start(bf16[2,16,2048]{2,1,0:T(8,128)(2,1)S(1)} %branch_0_fun.10.refs_0_), channel_id=1, source_target_pairs={{0,1},{1,2},{2,3},{3,0},{4,5},{5,6},{6,7},{7,4},{8,9},{9,10},{10,1... | collective-permute-start | bytes 393224 | tf_op jit(solution)/shard_map/cond/branch_0_fun/ppermute | solution.py:227
  79.1 1.8 %collective-permute-start.14 = (bf16[2,16,2048]{2,1,0:T(8,128)(2,1)S(1)}, bf16[2,16,2048]{2,1,0:T(8,128)(2,1)S(1)}, u32[]{:S(2)}, u32[]{:S(2)}) collective-permute-start(bf16[2,16,2048]{2,1,0:T(8,128)(2,1)S(1)} %collective-permute-done.8.refs_1_), channel_id=1, source_target_pairs={{0,2},{1,3},{2,0},{3,1},{4,6},{5,7},{6,4},{7,5},{8,10},{9,11},{10,... | collective-permute-start | bytes 393224 | tf_op jit(solution)/shard_map/cond/branch_0_fun/ppermute | solution.py:227
  80.9 0.6 collective-permute-start.12
  81.7 2.2 %collective-permute-start.10 = (bf16[2,16,2048]{2,1,0:T(8,128)(2,1)S(1)}, bf16[2,16,2048]{2,1,0:T(8,128)(2,1)S(1)}, u32[]{:S(2)}, u32[]{:S(2)}) collective-permute-start(bf16[2,16,2048]{2,1,0:T(8,128)(2,1)S(1)} %collective-permute-done.8.refs_1_), channel_id=1, source_target_pairs={{0,3},{1,0},{2,1},{3,2},{4,7},{5,4},{6,5},{7,6},{8,11},{9,8},{10,9... | collective-permute-start | bytes 393224 | tf_op jit(solution)/shard_map/cond/branch_0_fun/ppermute | solution.py:227
  83.9 0.5 collective-permute-done.9.refs_2_
  84.5 2.1 %collective-permute-done.14.refs_7_ = bf16[2,16,2048]{2,1,0:T(8,128)(2,1)S(1)} collective-permute-done((bf16[2,16,2048]{2,1,0:T(8,128)(2,1)S(1)}, bf16[2,16,2048]{2,1,0:T(8,128)(2,1)S(1)}, u32[]{:S(2)}, u32[]{:S(2)}) %collective-permute-start.14) | collective-permute-done | bytes 131104 | tf_op jit(solution)/shard_map/cond/branch_0_fun/ppermute | solution.py:227
  86.6 3.9 %collective-permute-done.12.refs_5_ = bf16[2,16,2048]{2,1,0:T(8,128)(2,1)S(1)} collective-permute-done((bf16[2,16,2048]{2,1,0:T(8,128)(2,1)S(1)}, bf16[2,16,2048]{2,1,0:T(8,128)(2,1)S(1)}, u32[]{:S(2)}, u32[]{:S(2)}) %collective-permute-start.12) | collective-permute-done | bytes 131104 | tf_op jit(solution)/shard_map/cond/branch_0_fun/ppermute | solution.py:227
  90.5 4.7 %branch_0_fun.11 = bf16[512,896]{1,0:T(8,128)(2,1)S(1)} custom-call(s32[2]{0:T(128)S(1)} %get-tuple-element.50.full_ref, s32[2]{0:T(128)S(1)} %get-tuple-element.52.me_ref, f32[512,128]{1,0:T(8,128)S(1)} %get-tuple-element.53.info_ref, bf16[2,16,2048]{2,1,0:T(8,128)(2,1)S(1)} %branch_0_fun.10.refs_0_, ...), custom_call_target="tpu_custom_call" | custom-call | flops 939524096 | bytes 8388608 | tf_op jit(solution)/shard_map/cond/branch_0_fun/pallas_call | solution.py:292
  95.7 32.0 %all_to_all.10 = bf16[128,4,896]{2,1,0:T(4,128)(2,1)S(1)} all-to-all(bf16[128,4,896]{2,1,0:T(4,128)(2,1)S(1)} %reshape.17), channel_id=1, replica_groups=mesh['exp'=16,'fsdp'=8] {'exp','fsdp'}, dimensions={0} | all-to-all | bytes 1835008 | tf_op jit(solution)/shard_map/all_to_all | solution.py:339
  127.6 1.0 reduce_sum.22
  (28 shorter events, 2.3 us)
Async XLA Ops:
  0.0 0.8 copy-start
  0.8 0.7 copy-start.1
  1.5 0.7 copy-start.2
  3.4 29.5 %all-to-all-start = ((bf16[128,4,1024]{2,1,0:T(4,128)(2,1)}), bf16[128,4,1024]{2,1,0:T(4,128)(2,1)S(1)}, u32[]{:S(2)}, u32[]{:S(2)}) async-start(bf16[128,4,1024]{2,1,0:T(4,128)(2,1)} %bitcast.2), calls=%async_computation | async-start | bytes 2097152 | tf_op jit(solution)/shard_map/all_to_all | solution.py:319
  37.1 7.4 %copy-start.3 = (bf16[2,896,2048]{2,1,0:T(8,128)(2,1)S(1)}, bf16[2,896,2048]{2,1,0:T(8,128)(2,1)}, u32[]{:S(2)}) copy-start(bf16[2,896,2048]{2,1,0:T(8,128)(2,1)} %get-tuple-element.58.weight_ref) | copy-start | bytes 22020100 | tf_op jit(solution)/shard_map/cond
  37.1 53.4 %slice-start = ((s8[7340032]{0:T(1024)(128)(4,1)}), s8[4194304]{0:T(1024)(128)(4,1)S(1)}, s32[]{:S(2)}) async-start(s8[7340032]{0:T(1024)(128)(4,1)} %bitcast.7), calls=%async_computation.2 | async-start | bytes 8388608 | tf_op jit(solution)/shard_map/cond
  42.6 20.3 %collective-permute-start.4 = (bf16[4,2,16,2048]{3,2,1,0:T(8,128)(2,1)S(1)}, bf16[4,2,16,2048]{3,2,1,0:T(8,128)(2,1)S(1)}, u32[]{:S(2)}, u32[]{:S(2)}) collective-permute-start(bf16[4,2,16,2048]{3,2,1,0:T(8,128)(2,1)S(1)} %get-tuple-element.66), channel_id=1, source_target_pairs={{0,4},{1,5},{2,6},{3,7},{4,0},{5,1},{6,2},{7,3},{8,12},{9,13},{10,... | collective-permute-start | bytes 1572872 | tf_op jit(solution)/shard_map/cond/branch_0_fun/ppermute | solution.py:231
  44.5 46.0 %slice-start.1 = ((s8[7340032]{0:T(1024)(128)(4,1)}), s8[3145728]{0:T(1024)(128)(4,1)S(1)}, s32[]{:S(2)}) async-start(s8[7340032]{0:T(1024)(128)(4,1)} %bitcast.7), calls=%async_computation.3 | async-start | bytes 6291456 | tf_op jit(solution)/shard_map/cond
  47.3 7.6 %collective-permute-start = (bf16[2,2,16,2048]{3,2,1,0:T(8,128)(2,1)S(1)}, bf16[2,2,16,2048]{3,2,1,0:T(8,128)(2,1)S(1)}, u32[]{:S(2)}, u32[]{:S(2)}) collective-permute-start(bf16[2,2,16,2048]{3,2,1,0:T(8,128)(2,1)S(1)} %get-tuple-element.60), channel_id=1, source_target_pairs={{0,1},{1,2},{2,3},{3,0},{4,5},{5,6},{6,7},{7,4},{8,9},{9,10},{10,1... | collective-permute-start | bytes 786440 | tf_op jit(solution)/shard_map/cond/branch_0_fun/ppermute | solution.py:227
  47.7 7.2 %collective-permute-start.1 = (bf16[2,2,16,2048]{3,2,1,0:T(8,128)(2,1)S(1)}, bf16[2,2,16,2048]{3,2,1,0:T(8,128)(2,1)S(1)}, u32[]{:S(2)}, u32[]{:S(2)}) collective-permute-start(bf16[2,2,16,2048]{3,2,1,0:T(8,128)(2,1)S(1)} %get-tuple-element.61), channel_id=1, source_target_pairs={{0,3},{1,0},{2,1},{3,2},{4,7},{5,4},{6,5},{7,6},{8,11},{9,8},{10,9... | collective-permute-start | bytes 786440 | tf_op jit(solution)/shard_map/cond/branch_0_fun/ppermute | solution.py:227
  50.0 12.4 %collective-permute-start.2 = (bf16[2,2,16,2048]{3,2,1,0:T(8,128)(2,1)S(1)}, bf16[2,2,16,2048]{3,2,1,0:T(8,128)(2,1)S(1)}, u32[]{:S(2)}, u32[]{:S(2)}) collective-permute-start(bf16[2,2,16,2048]{3,2,1,0:T(8,128)(2,1)S(1)} %get-tuple-element.62), channel_id=1, source_target_pairs={{0,2},{1,3},{2,0},{3,1},{4,6},{5,7},{6,4},{7,5},{8,10},{9,11},{10,... | collective-permute-start | bytes 786440 | tf_op jit(solution)/shard_map/cond/branch_0_fun/ppermute | solution.py:227
  62.8 6.3 %collective-permute-start.3 = (bf16[2,16,2048]{2,1,0:T(8,128)(2,1)S(1)}, bf16[2,16,2048]{2,1,0:T(8,128)(2,1)S(1)}, u32[]{:S(2)}, u32[]{:S(2)}) collective-permute-start(bf16[2,16,2048]{2,1,0:T(8,128)(2,1)S(1)} %get-tuple-element.64), channel_id=1, source_target_pairs={{0,4},{1,5},{2,6},{3,7},{4,0},{5,1},{6,2},{7,3},{8,12},{9,13},{10,... | collective-permute-start | bytes 393224 | tf_op jit(solution)/shard_map/cond/branch_0_fun/ppermute | solution.py:231
  63.4 5.7 %collective-permute-start.5 = (bf16[2,16,2048]{2,1,0:T(8,128)(2,1)S(1)}, bf16[2,16,2048]{2,1,0:T(8,128)(2,1)S(1)}, u32[]{:S(2)}, u32[]{:S(2)}) collective-permute-start(bf16[2,16,2048]{2,1,0:T(8,128)(2,1)S(1)} %get-tuple-element.68), channel_id=1, source_target_pairs={{0,1},{1,2},{2,3},{3,0},{4,5},{5,6},{6,7},{7,4},{8,9},{9,10},{10,1... | collective-permute-start | bytes 393224 | tf_op jit(solution)/shard_map/cond/branch_0_fun/ppermute | solution.py:227
  63.7 5.7 %collective-permute-start.6 = (bf16[2,16,2048]{2,1,0:T(8,128)(2,1)S(1)}, bf16[2,16,2048]{2,1,0:T(8,128)(2,1)S(1)}, u32[]{:S(2)}, u32[]{:S(2)}) collective-permute-start(bf16[2,16,2048]{2,1,0:T(8,128)(2,1)S(1)} %get-tuple-element.69), channel_id=1, source_target_pairs={{0,3},{1,0},{2,1},{3,2},{4,7},{5,4},{6,5},{7,6},{8,11},{9,8},{10,9... | collective-permute-start | bytes 393224 | tf_op jit(solution)/shard_map/cond/branch_0_fun/ppermute | solution.py:227
  66.1 6.3 %collective-permute-start.7 = (bf16[2,16,2048]{2,1,0:T(8,128)(2,1)S(1)}, bf16[2,16,2048]{2,1,0:T(8,128)(2,1)S(1)}, u32[]{:S(2)}, u32[]{:S(2)}) collective-permute-start(bf16[2,16,2048]{2,1,0:T(8,128)(2,1)S(1)} %get-tuple-element.70), channel_id=1, source_target_pairs={{0,2},{1,3},{2,0},{3,1},{4,6},{5,7},{6,4},{7,5},{8,10},{9,11},{10,... | collective-permute-start | bytes 393224 | tf_op jit(solution)/shard_map/cond/branch_0_fun/ppermute | solution.py:227
  72.7 6.4 %collective-permute-start.8 = (bf16[2,16,2048]{2,1,0:T(8,128)(2,1)S(1)}, bf16[2,16,2048]{2,1,0:T(8,128)(2,1)S(1)}, u32[]{:S(2)}, u32[]{:S(2)}) collective-permute-start(bf16[2,16,2048]{2,1,0:T(8,128)(2,1)S(1)} %branch_0_fun.10.refs_0_), channel_id=1, source_target_pairs={{0,4},{1,5},{2,6},{3,7},{4,0},{5,1},{6,2},{7,3},{8,12},{9,13},{10,... | collective-permute-start | bytes 393224 | tf_op jit(solution)/shard_map/cond/branch_0_fun/ppermute | solution.py:231
  76.3 5.4 %collective-permute-start.13 = (bf16[2,16,2048]{2,1,0:T(8,128)(2,1)S(1)}, bf16[2,16,2048]{2,1,0:T(8,128)(2,1)S(1)}, u32[]{:S(2)}, u32[]{:S(2)}) collective-permute-start(bf16[2,16,2048]{2,1,0:T(8,128)(2,1)S(1)} %branch_0_fun.10.refs_0_), channel_id=1, source_target_pairs={{0,2},{1,3},{2,0},{3,1},{4,6},{5,7},{6,4},{7,5},{8,10},{9,11},{10,... | collective-permute-start | bytes 393224 | tf_op jit(solution)/shard_map/cond/branch_0_fun/ppermute | solution.py:227
  76.3 7.6 %collective-permute-start.11 = (bf16[2,16,2048]{2,1,0:T(8,128)(2,1)S(1)}, bf16[2,16,2048]{2,1,0:T(8,128)(2,1)S(1)}, u32[]{:S(2)}, u32[]{:S(2)}) collective-permute-start(bf16[2,16,2048]{2,1,0:T(8,128)(2,1)S(1)} %branch_0_fun.10.refs_0_), channel_id=1, source_target_pairs={{0,1},{1,2},{2,3},{3,0},{4,5},{5,6},{6,7},{7,4},{8,9},{9,10},{10,1... | collective-permute-start | bytes 393224 | tf_op jit(solution)/shard_map/cond/branch_0_fun/ppermute | solution.py:227
  79.1 5.4 %collective-permute-start.9 = (bf16[2,16,2048]{2,1,0:T(8,128)(2,1)S(1)}, bf16[2,16,2048]{2,1,0:T(8,128)(2,1)S(1)}, u32[]{:S(2)}, u32[]{:S(2)}) collective-permute-start(bf16[2,16,2048]{2,1,0:T(8,128)(2,1)S(1)} %branch_0_fun.10.refs_0_), channel_id=1, source_target_pairs={{0,3},{1,0},{2,1},{3,2},{4,7},{5,4},{6,5},{7,6},{8,11},{9,8},{10,9... | collective-permute-start | bytes 393224 | tf_op jit(solution)/shard_map/cond/branch_0_fun/ppermute | solution.py:227
  79.1 7.5 %collective-permute-start.14 = (bf16[2,16,2048]{2,1,0:T(8,128)(2,1)S(1)}, bf16[2,16,2048]{2,1,0:T(8,128)(2,1)S(1)}, u32[]{:S(2)}, u32[]{:S(2)}) collective-permute-start(bf16[2,16,2048]{2,1,0:T(8,128)(2,1)S(1)} %collective-permute-done.8.refs_1_), channel_id=1, source_target_pairs={{0,2},{1,3},{2,0},{3,1},{4,6},{5,7},{6,4},{7,5},{8,10},{9,11},{10,... | collective-permute-start | bytes 393224 | tf_op jit(solution)/shard_map/cond/branch_0_fun/ppermute | solution.py:227
  80.9 9.6 %collective-permute-start.12 = (bf16[2,16,2048]{2,1,0:T(8,128)(2,1)S(1)}, bf16[2,16,2048]{2,1,0:T(8,128)(2,1)S(1)}, u32[]{:S(2)}, u32[]{:S(2)}) collective-permute-start(bf16[2,16,2048]{2,1,0:T(8,128)(2,1)S(1)} %collective-permute-done.8.refs_1_), channel_id=1, source_target_pairs={{0,1},{1,2},{2,3},{3,0},{4,5},{5,6},{6,7},{7,4},{8,9},{9,10},{10,1... | collective-permute-start | bytes 393224 | tf_op jit(solution)/shard_map/cond/branch_0_fun/ppermute | solution.py:227
  81.7 8.8 %collective-permute-start.10 = (bf16[2,16,2048]{2,1,0:T(8,128)(2,1)S(1)}, bf16[2,16,2048]{2,1,0:T(8,128)(2,1)S(1)}, u32[]{:S(2)}, u32[]{:S(2)}) collective-permute-start(bf16[2,16,2048]{2,1,0:T(8,128)(2,1)S(1)} %collective-permute-done.8.refs_1_), channel_id=1, source_target_pairs={{0,3},{1,0},{2,1},{3,2},{4,7},{5,4},{6,5},{7,6},{8,11},{9,8},{10,9... | collective-permute-start | bytes 393224 | tf_op jit(solution)/shard_map/cond/branch_0_fun/ppermute | solution.py:227

commit v3 on v2

--- a/solution.py
+++ b/solution.py
@@ -24,7 +24,17 @@
     rows, width = tokens.shape
     depth = width // fsdp_count
 
-    def body(tokens_ref, ids_ref, weight_ref, out_ref):
+    def body(tokens_hbm, ids_hbm, weight_hbm, out_ref, tokens_ref, ids_ref, weight_ref, sems):
+        moves = [
+            pltpu.make_async_copy(source, target, sems.at[index])
+            for index, (source, target) in enumerate(
+                ((ids_hbm, ids_ref), (weight_hbm, weight_ref), (tokens_hbm, tokens_ref))
+            )
+        ]
+        for move in moves:
+            move.start()
+        for move in moves:
+            move.wait()
         ids, weight = ids_ref[...], weight_ref[...]
         gates = ROUTE_SCALE * weight / jnp.sum(weight, axis=1, keepdims=True)
         column = lax.broadcasted_iota(jnp.int32, (rows, META), 1)
@@ -45,7 +55,14 @@
     return pl.pallas_call(
         body,
         out_shape=jax.ShapeDtypeStruct((exp_count, fsdp_count, rows, depth + META), jnp.bfloat16),
-        compiler_params=params(32),
+        in_specs=[pl.BlockSpec(memory_space=pltpu.HBM)] * 3,
+        scratch_shapes=[
+            pltpu.VMEM(tokens.shape, tokens.dtype),
+            pltpu.VMEM(expert_ids.shape, expert_ids.dtype),
+            pltpu.VMEM(combine_weight.shape, combine_weight.dtype),
+            pltpu.SemaphoreType.DMA((3,)),
+        ],
+        compiler_params=params(60),
     )(tokens, expert_ids, combine_weight)
 
 
@@ -117,9 +134,12 @@
             value = value.reshape(2 * RING, part, tile)
             for order in range(RING):
                 if z_first:
-                    sent, kept = outs
+                    sent, own, kept = outs
                     kept[order, unit, :, column] = value[2 * order]
-                    sent[order, unit, :, column] = value[2 * order + 1]
+                    if order == 0:
+                        own[unit, :, column] = value[1]
+                    else:
+                        sent[order - 1, unit, :, column] = value[2 * order + 1]
                 else:
                     outs[order][:, unit, :, column] = value[2 * order : 2 * order + 2]
 
@@ -135,7 +155,8 @@
                 put(local, value[:UNIT])
                 put(extra_unit(units, experts, local), value[UNIT:])
 
-    shapes = [(RING, units, part, width)] * 2 if z_first else [(2, units, part, width)] * RING
+    block = (units, part, width)
+    shapes = [(RING - 1,) + block, block, (RING,) + block] if z_first else [(2,) + block] * RING
     return pl.pallas_call(
         body,
         grid=(width // tile, experts),
@@ -186,12 +207,12 @@
         for order, out_ref in enumerate(outs):
 
             def piece(unit, column):
-                total = wide(kept_ref[order, unit, :, column]) + wide(came_ref[order, unit, :, column])
+                total = wide(kept_ref[order + 1, unit, :, column]) + wide(came_ref[order, unit, :, column])
                 out_ref[unit, :, column] = total.astype(jnp.bfloat16)
 
             in_pieces(block, 512, piece)
 
-    return whole_call(body, [(block, jnp.bfloat16)] * RING, kept, came)
+    return whole_call(body, [(block, jnp.bfloat16)] * (RING - 1), kept, came)
 
 
 def add_along(*terms):
@@ -209,18 +230,18 @@
     return whole_call(body, [(block, jnp.bfloat16), (block, jnp.float32)], *terms)
 
 
-def activate(stays, came, *terms):
+def activate(stays, came, kept, *terms):
     block = stays.shape
 
-    def body(stays_ref, came_ref, *refs):
+    def body(stays_ref, came_ref, kept_ref, *refs):
         def piece(unit, column):
             gate = stays_ref[unit, :, column] + wide(came_ref[unit, :, column])
-            up = sum(wide(ref[unit, :, column]) for ref in refs[1:-1]) + wide(refs[0][unit, :, column])
+            up = sum(wide(ref[unit, :, column]) for ref in refs[:-1]) + wide(kept_ref[0, unit, :, column])
             refs[-1][unit, :, column] = (gate / (1.0 + jnp.exp(-gate)) * up).astype(jnp.bfloat16)
 
         in_pieces(block, 512, piece)
 
-    return whole_call(body, [(block, jnp.bfloat16)], stays, came, *terms)[0]
+    return whole_call(body, [(block, jnp.bfloat16)], stays, came, kept, *terms)[0]
 
 
 def along(value, step):
@@ -231,12 +252,8 @@
     return lax.ppermute(value, "fsdp", [(i, (i + RING) % (2 * RING)) for i in range(2 * RING)])
 
 
-def to_others(kept, right, left, far):
-    return kept, along(right, 1), along(left, -1), along(far, 2)
-
-
-def from_others(value):
-    return along(value, -1), along(value, 1), along(value, 2)
+def to_others(right, left, far):
+    return along(right, 1), along(left, -1), along(far, 2)
 
 
 def finish(full, me, info, parts, down_weight, tile):
@@ -321,21 +338,27 @@
     packed, info, full = gather_rows(me, rows_in, experts, exp_count * experts, 2 * UNIT)
 
     def routed(units, full, packed, info, gate_weight, up_weight, down_weight):
-        sent, kept = project(full, packed, up_weight, units, True, 1024)
+        sent, own, kept = project(full, packed, up_weight, units, True, 1024)
         packed, sent = lax.optimization_barrier((packed, sent))
-        gate_terms = project(full, packed, gate_weight, units, False, 1024)
+        gate_kept, *gate_terms = project(full, packed, gate_weight, units, False, 1024)
         came = across(sent)
-        sent, stays = add_along(*to_others(*gate_terms))
-        up_terms = to_others(*fold(kept, came))
-        hidden = activate(stays, across(sent), *up_terms)
+        own = across(own)
+        gate_terms = to_others(*gate_terms)
+        up_terms = fold(kept, came)
+        gate_kept, up_terms = lax.optimization_barrier((gate_kept, up_terms))
+        up_terms = to_others(*up_terms)
+        sent, stays = add_along(gate_kept, *gate_terms)
+        hidden = activate(stays, across(sent), kept, own, *up_terms)
         other = across(hidden)
-        right, left, far = from_others(hidden)
-        right_other, left_other, far_other = from_others(other)
+        right, left, far = along(hidden, -1), along(hidden, 1), along(hidden, 2)
+        right_other, left_other, far_other = along(other, -1), along(other, 1), across(far)
         parts = hidden, other, right, right_other, left, left_other, far, far_other
         return finish(full, me, info, parts, down_weight, 448)
 
-    branches = [lambda *operands, units=units: routed(units, *operands) for units in range(experts, 2 * experts + 1)]
-    mixed = lax.switch(jnp.sum(full), branches, full, packed, info, gate_weight, up_weight, down_weight)
+    order = (experts + 1, experts + 2, experts)
+    branches = [lambda *operands, units=units: routed(units, *operands) for units in order]
+    number = (jnp.sum(full) + len(order) - 1) % len(order)
+    mixed = lax.switch(number, branches, full, packed, info, gate_weight, up_weight, down_weight)
     home = lax.all_to_all(mixed.reshape(devices, rows_dev, depth), BOTH, 0, 0, tiled=True)
     home = home.reshape(exp_count, fsdp_count, rows_dev, depth).astype(jnp.float32)
     return jnp.sum(home, axis=0).astype(jnp.bfloat16).transpose(1, 0, 2).reshape(rows_dev, width)

time: 129 us -> 126 us (0.977)
  waiting for transfers between devices: 42.9 us -> 37.2 us
  local copies, waits for them, and re-layouts: 2.67 us -> 0.49 us
  starting transfers between devices: 30.5 us -> 32.4 us
  blocking collectives: 32 us -> 33.7 us
    ppermute x12 -> x11, waiting for transfers between devices: 22.1 us -> 13.9 us  [along(): lax.ppermute(value, 'fsdp', [(i, i // RING * RING + (i + step) % RING) fo...]
    ppermute x3 -> x5, starting transfers between devices: 5.61 us -> 9.3 us  [across(): lax.ppermute(value, 'fsdp', [(i, (i + RING) % (2 * RING)) for i in range(...]
    ppermute x3 -> x5, waiting for transfers between devices: 2.94 us -> 5.39 us  [across(): lax.ppermute(value, 'fsdp', [(i, (i + RING) % (2 * RING)) for i in range(...]
    unnamed x6 -> x0, local copies, waits for them, and re-layouts: 2.18 us -> none
    ppermute x12 -> x11, starting transfers between devices: 13.3 us -> 11.6 us  [along(): lax.ppermute(value, 'fsdp', [(i, i // RING * RING + (i + step) % RING) fo...]
    all_to_all x1, blocking collectives: 32 us -> 33.7 us  [on_device(): lax.all_to_all(mixed.reshape(devices, rows_dev, depth), BOTH, 0, 0, tiled...]
  transfers between devices with their start and end apart: 16 -> 17, of which waited for: 10 -> 7; matrix products, arithmetic and copies ran while one was open for 0% -> 0% of each run, Pallas kernels for 3% -> 3%
where the time goes in v3:
time: 126 us
  waiting for transfers between devices  37.2 us (30%)
  blocking collectives  33.7 us (27%)
  starting transfers between devices  32.4 us (26%)
  Pallas kernels  18.6 us (15%)
  other arithmetic  1.72 us (1%)
    all_to_all x1, blocking collectives, on_device(): lax.all_to_all(mixed.reshape(devices, rows_dev, depth), BOTH, 0, 0, tiled...  33.7 us
    all_to_all x1, waiting for transfers between devices, on_device(): lax.all_to_all(sent, BOTH, 0, 0, tiled=True)  17.9 us
    ppermute x11, waiting for transfers between devices, along(): lax.ppermute(value, 'fsdp', [(i, i // RING * RING + (i + step) % RING) fo...  13.9 us
    ppermute x11, starting transfers between devices, along(): lax.ppermute(value, 'fsdp', [(i, i // RING * RING + (i + step) % RING) fo...  11.6 us
    all_to_all x1, starting transfers between devices, on_device(): lax.all_to_all(sent, BOTH, 0, 0, tiled=True)  11.5 us
    ppermute x5, starting transfers between devices, across(): lax.ppermute(value, 'fsdp', [(i, (i + RING) % (2 * RING)) for i in range(...  9.3 us
    pallas_call x2, Pallas kernels, project(): pl.pallas_call(body, grid=(width // tile, experts), out_shape=tuple((jax....  8.33 us
    ppermute x5, waiting for transfers between devices, across(): lax.ppermute(value, 'fsdp', [(i, (i + RING) % (2 * RING)) for i in range(...  5.39 us
  transfers between devices with their start and end apart: 17, of which 7 were waited for; matrix products, arithmetic and copies ran while one was open for 0% of the time, Pallas kernels for 3%

profile of v3, /device:TPU:1, one launch (start us, length us, event | category | flops | bytes accessed | tf_op | source)
XLA Modules:
  0.0 125.5 jit_solution(13874510977784440852)
XLA Ops:
  0.0 2.1 %shard_map.64 = bf16[16,8,4,1024]{3,2,1,0:T(4,128)(2,1)} custom-call(bf16[4,7168]{1,0:T(4,128)(2,1)} %tokens_hbm.1, s32[4,8]{1,0:T(4,128)} %ids_hbm.1, f32[4,8]{1,0:T(4,128)} %weight_hbm.1), custom_call_target="tpu_custom_call" | custom-call | tf_op jit(solution)/shard_map/pallas_call | solution.py:55
  2.1 11.5 %all-to-all-start = ((bf16[128,4,1024]{2,1,0:T(4,128)(2,1)}), bf16[128,4,1024]{2,1,0:T(4,128)(2,1)S(1)}, u32[]{:S(2)}, u32[]{:S(2)}) async-start(bf16[128,4,1024]{2,1,0:T(4,128)(2,1)} %bitcast.13), calls=%async_computation | async-start | bytes 2097152 | tf_op jit(solution)/shard_map/all_to_all | solution.py:336
  13.7 17.9 %all-to-all-done = bf16[128,4,1024]{2,1,0:T(4,128)(2,1)S(1)} async-done(((bf16[128,4,1024]{2,1,0:T(4,128)(2,1)}), bf16[128,4,1024]{2,1,0:T(4,128)(2,1)S(1)}, u32[]{:S(2)}, u32[]{:S(2)}) %all-to-all-start) | async-done | bytes 1048608 | tf_op jit(solution)/shard_map/all_to_all | solution.py:336
  31.7 0.3 reshape.16.rows_ref
  31.9 2.5 %shard_map.65 = (bf16[2,256,896]{2,1,0:T(8,128)(2,1)S(1)}, f32[512,128]{1,0:T(8,128)S(1)}, s32[2]{0:T(128)S(1)}) custom-call(s32[2]{0:T(128)S(1)} %pad_add_fusion.me_ref, bf16[512,1024]{1,0:T(8,128)(2,1)S(1)} %reshape.16.rows_ref), custom_call_target="tpu_custom_call" | custom-call | tf_op jit(solution)/shard_map/pallas_call | solution.py:103
  34.5 0.6 reduce_sum.21
  35.8 54.8 %conditional.1 = (bf16[512,896]{1,0:T(8,128)(2,1)S(1)}) conditional(s32[]{:T(128)} %clamp.3, (s32[2]{0:T(128)S(1)}, bf16[2,256,896]{2,1,0:T(8,128)(2,1)S(1)}, bf16[2,896,2048]{2,1,0:T(8,128)(2,1)}, bf16[2,896,2048]{2,1,0:T(8,128)(2,1)}, s32[2]{0:T(128)S(1)}, /*index=5*/f32[512,128]{1,0:T(8,128)S(1)}, ...), branch_computations={%region_1.2_spmd, %region_2.3_spmd, %region_3.4_spmd} | conditional | flops 5637144576 | bytes 101712592 | solution.py:361
  36.0 5.5 %branch_2_fun.6 = (bf16[3,2,16,2048]{3,2,1,0:T(8,128)(2,1)S(1)}, bf16[2,16,2048]{2,1,0:T(8,128)(2,1)S(1)}, bf16[4,2,16,2048]{3,2,1,0:T(8,128)(2,1)S(1)}) custom-call(s32[2]{0:T(128)S(1)} %get-tuple-element.101.full_ref, bf16[2,256,896]{2,1,0:T(8,128)(2,1)S(1)} %get-tuple-element.107.packed_ref, bf16[2,896,2048]{2,1,0:T(8,128)(2,1)} %get-tuple-element.105.weight_ref), custom_call_target="tpu_custom_call" | custom-call | flops 939524096 | bytes 8388608 | tf_op jit(solution)/shard_map/cond/branch_2_fun/pallas_call | solution.py:160
  41.5 1.9 %collective-permute-start.32 = (bf16[3,2,16,2048]{3,2,1,0:T(8,128)(2,1)S(1)}, bf16[3,2,16,2048]{3,2,1,0:T(8,128)(2,1)S(1)}, u32[]{:S(2)}, u32[]{:S(2)}) collective-permute-start(bf16[3,2,16,2048]{3,2,1,0:T(8,128)(2,1)S(1)} %get-tuple-element.111), channel_id=1, source_target_pairs={{0,4},{1,5},{2,6},{3,7},{4,0},{5,1},{6,2},{7,3},{8,12},{9,13},{10,... | collective-permute-start | bytes 1179656 | tf_op jit(solution)/shard_map/cond/branch_2_fun/ppermute | solution.py:252
  43.4 2.8 %branch_2_fun.7 = (bf16[2,2,16,2048]{3,2,1,0:T(8,128)(2,1)S(1)}, bf16[2,2,16,2048]{3,2,1,0:T(8,128)(2,1)S(1)}, bf16[2,2,16,2048]{3,2,1,0:T(8,128)(2,1)S(1)}, bf16[2,2,16,2048]{3,2,1,0:T(8,128)(2,1)S(1)}) custom-call(s32[2]{0:T(128)S(1)} %get-tuple-element.101.full_ref, bf16[2,256,896]{2,1,0:T(8,128)(2,1)S(1)} %get-tuple-element.107.packed_ref, ...), custom_call_target="tpu_custom_call" | custom-call | flops 939524096 | bytes 8388608 | tf_op jit(solution)/shard_map/cond/branch_2_fun/pallas_call | solution.py:160
  46.3 0.4 collective-permute-start.33
  46.6 2.4 %collective-permute-start.34 = (bf16[2,2,16,2048]{3,2,1,0:T(8,128)(2,1)S(1)}, bf16[2,2,16,2048]{3,2,1,0:T(8,128)(2,1)S(1)}, u32[]{:S(2)}, u32[]{:S(2)}) collective-permute-start(bf16[2,2,16,2048]{3,2,1,0:T(8,128)(2,1)S(1)} %get-tuple-element.117), channel_id=1, source_target_pairs={{0,3},{1,0},{2,1},{3,2},{4,7},{5,4},{6,5},{7,6},{8,11},{9,8},{10,9... | collective-permute-start | bytes 786440 | tf_op jit(solution)/shard_map/cond/branch_2_fun/ppermute | solution.py:248
  49.0 0.5 collective-permute-start.35
  49.5 1.2 collective-permute-start.37
  50.7 2.0 %collective-permute-done.32.came_ref = bf16[3,2,16,2048]{3,2,1,0:T(8,128)(2,1)S(1)} collective-permute-done((bf16[3,2,16,2048]{3,2,1,0:T(8,128)(2,1)S(1)}, bf16[3,2,16,2048]{3,2,1,0:T(8,128)(2,1)S(1)}, u32[]{:S(2)}, u32[]{:S(2)}) %collective-permute-start.32) | collective-permute-done | bytes 393248 | tf_op jit(solution)/shard_map/cond/branch_2_fun/ppermute | solution.py:252
  52.7 0.3 branch_2_fun.8
  53.0 0.9 collective-permute-done.33.refs_1_
  53.9 7.6 %collective-permute-done.35.refs_3_ = bf16[2,2,16,2048]{3,2,1,0:T(8,128)(2,1)S(1)} collective-permute-done((bf16[2,2,16,2048]{3,2,1,0:T(8,128)(2,1)S(1)}, bf16[2,2,16,2048]{3,2,1,0:T(8,128)(2,1)S(1)}, u32[]{:S(2)}, u32[]{:S(2)}) %collective-permute-start.35) | collective-permute-done | bytes 262176 | tf_op jit(solution)/shard_map/cond/branch_2_fun/ppermute | solution.py:248
  61.4 0.3 branch_2_fun.9
  61.8 0.3 collective-permute-start.38
  62.1 2.4 %collective-permute-start.39 = (bf16[2,16,2048]{2,1,0:T(8,128)(2,1)S(1)}, bf16[2,16,2048]{2,1,0:T(8,128)(2,1)S(1)}, u32[]{:S(2)}, u32[]{:S(2)}) collective-permute-start(bf16[2,16,2048]{2,1,0:T(8,128)(2,1)S(1)} %get-tuple-element.123), channel_id=1, source_target_pairs={{0,3},{1,0},{2,1},{3,2},{4,7},{5,4},{6,5},{7,6},{8,11},{9,8},{10,9... | collective-permute-start | bytes 393224 | tf_op jit(solution)/shard_map/cond/branch_2_fun/ppermute | solution.py:248
  64.6 3.4 %collective-permute-done.36.came_ref = bf16[2,16,2048]{2,1,0:T(8,128)(2,1)S(1)} collective-permute-done((bf16[2,16,2048]{2,1,0:T(8,128)(2,1)S(1)}, bf16[2,16,2048]{2,1,0:T(8,128)(2,1)S(1)}, u32[]{:S(2)}, u32[]{:S(2)}) %collective-permute-start.36) | collective-permute-done | bytes 131104 | tf_op jit(solution)/shard_map/cond/branch_2_fun/ppermute | solution.py:252
  68.0 2.9 %collective-permute-done.40.refs_3_ = bf16[2,16,2048]{2,1,0:T(8,128)(2,1)S(1)} collective-permute-done((bf16[2,16,2048]{2,1,0:T(8,128)(2,1)S(1)}, bf16[2,16,2048]{2,1,0:T(8,128)(2,1)S(1)}, u32[]{:S(2)}, u32[]{:S(2)}) %collective-permute-start.40) | collective-permute-done | bytes 131104 | tf_op jit(solution)/shard_map/cond/branch_2_fun/ppermute | solution.py:248
  70.9 0.3 branch_2_fun.10.refs_0_
  71.4 3.5 %collective-permute-start.41 = (bf16[2,16,2048]{2,1,0:T(8,128)(2,1)S(1)}, bf16[2,16,2048]{2,1,0:T(8,128)(2,1)S(1)}, u32[]{:S(2)}, u32[]{:S(2)}) collective-permute-start(bf16[2,16,2048]{2,1,0:T(8,128)(2,1)S(1)} %branch_2_fun.10.refs_0_), channel_id=1, source_target_pairs={{0,4},{1,5},{2,6},{3,7},{4,0},{5,1},{6,2},{7,3},{8,12},{9,13},{10,... | collective-permute-start | bytes 393224 | tf_op jit(solution)/shard_map/cond/branch_2_fun/ppermute | solution.py:252
  74.9 2.6 %collective-permute-start.44 = (bf16[2,16,2048]{2,1,0:T(8,128)(2,1)S(1)}, bf16[2,16,2048]{2,1,0:T(8,128)(2,1)S(1)}, u32[]{:S(2)}, u32[]{:S(2)}) collective-permute-start(bf16[2,16,2048]{2,1,0:T(8,128)(2,1)S(1)} %branch_2_fun.10.refs_0_), channel_id=1, source_target_pairs={{0,1},{1,2},{2,3},{3,0},{4,5},{5,6},{6,7},{7,4},{8,9},{9,10},{10,1... | collective-permute-start | bytes 393224 | tf_op jit(solution)/shard_map/cond/branch_2_fun/ppermute | solution.py:248
  77.6 2.7 %collective-permute-start.47 = (bf16[2,16,2048]{2,1,0:T(8,128)(2,1)S(1)}, bf16[2,16,2048]{2,1,0:T(8,128)(2,1)S(1)}, u32[]{:S(2)}, u32[]{:S(2)}) collective-permute-start(bf16[2,16,2048]{2,1,0:T(8,128)(2,1)S(1)} %collective-permute-done.46.refs_6_), channel_id=1, source_target_pairs={{0,4},{1,5},{2,6},{3,7},{4,0},{5,1},{6,2},{7,3},{8,12},{9,13},{10,... | collective-permute-start | bytes 393224 | tf_op jit(solution)/shard_map/cond/branch_2_fun/ppermute | solution.py:252
  80.2 2.7 %collective-permute-start.43 = (bf16[2,16,2048]{2,1,0:T(8,128)(2,1)S(1)}, bf16[2,16,2048]{2,1,0:T(8,128)(2,1)S(1)}, u32[]{:S(2)}, u32[]{:S(2)}) collective-permute-start(bf16[2,16,2048]{2,1,0:T(8,128)(2,1)S(1)} %collective-permute-done.41.refs_1_), channel_id=1, source_target_pairs={{0,3},{1,0},{2,1},{3,2},{4,7},{5,4},{6,5},{7,6},{8,11},{9,8},{10,9... | collective-permute-start | bytes 393224 | tf_op jit(solution)/shard_map/cond/branch_2_fun/ppermute | solution.py:248
  82.9 2.6 %collective-permute-done.45.refs_5_ = bf16[2,16,2048]{2,1,0:T(8,128)(2,1)S(1)} collective-permute-done((bf16[2,16,2048]{2,1,0:T(8,128)(2,1)S(1)}, bf16[2,16,2048]{2,1,0:T(8,128)(2,1)S(1)}, u32[]{:S(2)}, u32[]{:S(2)}) %collective-permute-start.45) | collective-permute-done | bytes 131104 | tf_op jit(solution)/shard_map/cond/branch_2_fun/ppermute | solution.py:248
  85.6 4.7 %branch_2_fun.11 = bf16[512,896]{1,0:T(8,128)(2,1)S(1)} custom-call(s32[2]{0:T(128)S(1)} %get-tuple-element.101.full_ref, s32[2]{0:T(128)S(1)} %get-tuple-element.102.me_ref, f32[512,128]{1,0:T(8,128)S(1)} %get-tuple-element.103.info_ref, bf16[2,16,2048]{2,1,0:T(8,128)(2,1)S(1)} %branch_2_fun.10.refs_0_, ...), custom_call_target="tpu_custom_call" | custom-call | flops 939524096 | bytes 8388608 | tf_op jit(solution)/shard_map/cond/branch_2_fun/pallas_call | solution.py:309
  90.8 33.7 %all_to_all.10 = bf16[128,4,896]{2,1,0:T(4,128)(2,1)S(1)} all-to-all(bf16[128,4,896]{2,1,0:T(4,128)(2,1)S(1)} %reshape.17), channel_id=1, replica_groups=mesh['exp'=16,'fsdp'=8] {'exp','fsdp'}, dimensions={0} | all-to-all | bytes 1835008 | tf_op jit(solution)/shard_map/all_to_all | solution.py:362
  124.5 1.0 reduce_sum.22
  (24 shorter events, 0.7 us)
Async XLA Ops:
  2.1 29.5 %all-to-all-start = ((bf16[128,4,1024]{2,1,0:T(4,128)(2,1)}), bf16[128,4,1024]{2,1,0:T(4,128)(2,1)S(1)}, u32[]{:S(2)}, u32[]{:S(2)}) async-start(bf16[128,4,1024]{2,1,0:T(4,128)(2,1)} %bitcast.13), calls=%async_computation | async-start | bytes 2097152 | tf_op jit(solution)/shard_map/all_to_all | solution.py:336
  36.0 7.4 %copy-start.2 = (bf16[2,896,2048]{2,1,0:T(8,128)(2,1)S(1)}, bf16[2,896,2048]{2,1,0:T(8,128)(2,1)}, u32[]{:S(2)}) copy-start(bf16[2,896,2048]{2,1,0:T(8,128)(2,1)} %get-tuple-element.108.weight_ref) | copy-start | bytes 22020100 | tf_op jit(solution)/shard_map/cond
  36.0 49.5 %slice-start.4 = ((s8[7340032]{0:T(1024)(128)(4,1)}), s8[4194304]{0:T(1024)(128)(4,1)S(1)}, s32[]{:S(2)}) async-start(s8[7340032]{0:T(1024)(128)(4,1)} %bitcast.11), calls=%async_computation.6 | async-start | bytes 8388608 | tf_op jit(solution)/shard_map/cond
  41.5 11.1 %collective-permute-start.32 = (bf16[3,2,16,2048]{3,2,1,0:T(8,128)(2,1)S(1)}, bf16[3,2,16,2048]{3,2,1,0:T(8,128)(2,1)S(1)}, u32[]{:S(2)}, u32[]{:S(2)}) collective-permute-start(bf16[3,2,16,2048]{3,2,1,0:T(8,128)(2,1)S(1)} %get-tuple-element.111), channel_id=1, source_target_pairs={{0,4},{1,5},{2,6},{3,7},{4,0},{5,1},{6,2},{7,3},{8,12},{9,13},{10,... | collective-permute-start | bytes 1179656 | tf_op jit(solution)/shard_map/cond/branch_2_fun/ppermute | solution.py:252
  43.4 42.2 %slice-start.5 = ((s8[7340032]{0:T(1024)(128)(4,1)}), s8[3145728]{0:T(1024)(128)(4,1)S(1)}, s32[]{:S(2)}) async-start(s8[7340032]{0:T(1024)(128)(4,1)} %bitcast.11), calls=%async_computation.7 | async-start | bytes 6291456 | tf_op jit(solution)/shard_map/cond
  46.3 7.6 %collective-permute-start.33 = (bf16[2,2,16,2048]{3,2,1,0:T(8,128)(2,1)S(1)}, bf16[2,2,16,2048]{3,2,1,0:T(8,128)(2,1)S(1)}, u32[]{:S(2)}, u32[]{:S(2)}) collective-permute-start(bf16[2,2,16,2048]{3,2,1,0:T(8,128)(2,1)S(1)} %get-tuple-element.116), channel_id=1, source_target_pairs={{0,1},{1,2},{2,3},{3,0},{4,5},{5,6},{6,7},{7,4},{8,9},{9,10},{10,1... | collective-permute-start | bytes 786440 | tf_op jit(solution)/shard_map/cond/branch_2_fun/ppermute | solution.py:248
  46.6 7.2 %collective-permute-start.34 = (bf16[2,2,16,2048]{3,2,1,0:T(8,128)(2,1)S(1)}, bf16[2,2,16,2048]{3,2,1,0:T(8,128)(2,1)S(1)}, u32[]{:S(2)}, u32[]{:S(2)}) collective-permute-start(bf16[2,2,16,2048]{3,2,1,0:T(8,128)(2,1)S(1)} %get-tuple-element.117), channel_id=1, source_target_pairs={{0,3},{1,0},{2,1},{3,2},{4,7},{5,4},{6,5},{7,6},{8,11},{9,8},{10,9... | collective-permute-start | bytes 786440 | tf_op jit(solution)/shard_map/cond/branch_2_fun/ppermute | solution.py:248
  49.0 12.4 %collective-permute-start.35 = (bf16[2,2,16,2048]{3,2,1,0:T(8,128)(2,1)S(1)}, bf16[2,2,16,2048]{3,2,1,0:T(8,128)(2,1)S(1)}, u32[]{:S(2)}, u32[]{:S(2)}) collective-permute-start(bf16[2,2,16,2048]{3,2,1,0:T(8,128)(2,1)S(1)} %get-tuple-element.118), channel_id=1, source_target_pairs={{0,2},{1,3},{2,0},{3,1},{4,6},{5,7},{6,4},{7,5},{8,10},{9,11},{10,... | collective-permute-start | bytes 786440 | tf_op jit(solution)/shard_map/cond/branch_2_fun/ppermute | solution.py:248
  49.5 15.1 %collective-permute-start.37 = (bf16[2,16,2048]{2,1,0:T(8,128)(2,1)S(1)}, bf16[2,16,2048]{2,1,0:T(8,128)(2,1)S(1)}, u32[]{:S(2)}, u32[]{:S(2)}) collective-permute-start(bf16[2,16,2048]{2,1,0:T(8,128)(2,1)S(1)} %get-tuple-element.121), channel_id=1, source_target_pairs={{0,4},{1,5},{2,6},{3,7},{4,0},{5,1},{6,2},{7,3},{8,12},{9,13},{10,... | collective-permute-start | bytes 393224 | tf_op jit(solution)/shard_map/cond/branch_2_fun/ppermute | solution.py:252
  61.7 6.3 %collective-permute-start.36 = (bf16[2,16,2048]{2,1,0:T(8,128)(2,1)S(1)}, bf16[2,16,2048]{2,1,0:T(8,128)(2,1)S(1)}, u32[]{:S(2)}, u32[]{:S(2)}) collective-permute-start(bf16[2,16,2048]{2,1,0:T(8,128)(2,1)S(1)} %get-tuple-element.120), channel_id=1, source_target_pairs={{0,4},{1,5},{2,6},{3,7},{4,0},{5,1},{6,2},{7,3},{8,12},{9,13},{10,... | collective-permute-start | bytes 393224 | tf_op jit(solution)/shard_map/cond/branch_2_fun/ppermute | solution.py:252
  61.8 6.2 %collective-permute-start.38 = (bf16[2,16,2048]{2,1,0:T(8,128)(2,1)S(1)}, bf16[2,16,2048]{2,1,0:T(8,128)(2,1)S(1)}, u32[]{:S(2)}, u32[]{:S(2)}) collective-permute-start(bf16[2,16,2048]{2,1,0:T(8,128)(2,1)S(1)} %get-tuple-element.122), channel_id=1, source_target_pairs={{0,1},{1,2},{2,3},{3,0},{4,5},{5,6},{6,7},{7,4},{8,9},{9,10},{10,1... | collective-permute-start | bytes 393224 | tf_op jit(solution)/shard_map/cond/branch_2_fun/ppermute | solution.py:248
  62.1 5.9 %collective-permute-start.39 = (bf16[2,16,2048]{2,1,0:T(8,128)(2,1)S(1)}, bf16[2,16,2048]{2,1,0:T(8,128)(2,1)S(1)}, u32[]{:S(2)}, u32[]{:S(2)}) collective-permute-start(bf16[2,16,2048]{2,1,0:T(8,128)(2,1)S(1)} %get-tuple-element.123), channel_id=1, source_target_pairs={{0,3},{1,0},{2,1},{3,2},{4,7},{5,4},{6,5},{7,6},{8,11},{9,8},{10,9... | collective-permute-start | bytes 393224 | tf_op jit(solution)/shard_map/cond/branch_2_fun/ppermute | solution.py:248
  64.6 6.3 %collective-permute-start.40 = (bf16[2,16,2048]{2,1,0:T(8,128)(2,1)S(1)}, bf16[2,16,2048]{2,1,0:T(8,128)(2,1)S(1)}, u32[]{:S(2)}, u32[]{:S(2)}) collective-permute-start(bf16[2,16,2048]{2,1,0:T(8,128)(2,1)S(1)} %get-tuple-element.124), channel_id=1, source_target_pairs={{0,2},{1,3},{2,0},{3,1},{4,6},{5,7},{6,4},{7,5},{8,10},{9,11},{10,... | collective-permute-start | bytes 393224 | tf_op jit(solution)/shard_map/cond/branch_2_fun/ppermute | solution.py:248
  71.2 6.4 %collective-permute-start.46 = (bf16[2,16,2048]{2,1,0:T(8,128)(2,1)S(1)}, bf16[2,16,2048]{2,1,0:T(8,128)(2,1)S(1)}, u32[]{:S(2)}, u32[]{:S(2)}) collective-permute-start(bf16[2,16,2048]{2,1,0:T(8,128)(2,1)S(1)} %branch_2_fun.10.refs_0_), channel_id=1, source_target_pairs={{0,2},{1,3},{2,0},{3,1},{4,6},{5,7},{6,4},{7,5},{8,10},{9,11},{10,... | collective-permute-start | bytes 393224 | tf_op jit(solution)/shard_map/cond/branch_2_fun/ppermute | solution.py:248
  71.4 8.9 %collective-permute-start.41 = (bf16[2,16,2048]{2,1,0:T(8,128)(2,1)S(1)}, bf16[2,16,2048]{2,1,0:T(8,128)(2,1)S(1)}, u32[]{:S(2)}, u32[]{:S(2)}) collective-permute-start(bf16[2,16,2048]{2,1,0:T(8,128)(2,1)S(1)} %branch_2_fun.10.refs_0_), channel_id=1, source_target_pairs={{0,4},{1,5},{2,6},{3,7},{4,0},{5,1},{6,2},{7,3},{8,12},{9,13},{10,... | collective-permute-start | bytes 393224 | tf_op jit(solution)/shard_map/cond/branch_2_fun/ppermute | solution.py:252
  74.9 8.0 %collective-permute-start.44 = (bf16[2,16,2048]{2,1,0:T(8,128)(2,1)S(1)}, bf16[2,16,2048]{2,1,0:T(8,128)(2,1)S(1)}, u32[]{:S(2)}, u32[]{:S(2)}) collective-permute-start(bf16[2,16,2048]{2,1,0:T(8,128)(2,1)S(1)} %branch_2_fun.10.refs_0_), channel_id=1, source_target_pairs={{0,1},{1,2},{2,3},{3,0},{4,5},{5,6},{6,7},{7,4},{8,9},{9,10},{10,1... | collective-permute-start | bytes 393224 | tf_op jit(solution)/shard_map/cond/branch_2_fun/ppermute | solution.py:248
  77.5 5.4 %collective-permute-start.42 = (bf16[2,16,2048]{2,1,0:T(8,128)(2,1)S(1)}, bf16[2,16,2048]{2,1,0:T(8,128)(2,1)S(1)}, u32[]{:S(2)}, u32[]{:S(2)}) collective-permute-start(bf16[2,16,2048]{2,1,0:T(8,128)(2,1)S(1)} %branch_2_fun.10.refs_0_), channel_id=1, source_target_pairs={{0,3},{1,0},{2,1},{3,2},{4,7},{5,4},{6,5},{7,6},{8,11},{9,8},{10,9... | collective-permute-start | bytes 393224 | tf_op jit(solution)/shard_map/cond/branch_2_fun/ppermute | solution.py:248
  77.6 5.3 %collective-permute-start.47 = (bf16[2,16,2048]{2,1,0:T(8,128)(2,1)S(1)}, bf16[2,16,2048]{2,1,0:T(8,128)(2,1)S(1)}, u32[]{:S(2)}, u32[]{:S(2)}) collective-permute-start(bf16[2,16,2048]{2,1,0:T(8,128)(2,1)S(1)} %collective-permute-done.46.refs_6_), channel_id=1, source_target_pairs={{0,4},{1,5},{2,6},{3,7},{4,0},{5,1},{6,2},{7,3},{8,12},{9,13},{10,... | collective-permute-start | bytes 393224 | tf_op jit(solution)/shard_map/cond/branch_2_fun/ppermute | solution.py:252
  80.2 5.3 %collective-permute-start.45 = (bf16[2,16,2048]{2,1,0:T(8,128)(2,1)S(1)}, bf16[2,16,2048]{2,1,0:T(8,128)(2,1)S(1)}, u32[]{:S(2)}, u32[]{:S(2)}) collective-permute-start(bf16[2,16,2048]{2,1,0:T(8,128)(2,1)S(1)} %collective-permute-done.41.refs_1_), channel_id=1, source_target_pairs={{0,1},{1,2},{2,3},{3,0},{4,5},{5,6},{6,7},{7,4},{8,9},{9,10},{10,1... | collective-permute-start | bytes 393224 | tf_op jit(solution)/shard_map/cond/branch_2_fun/ppermute | solution.py:248
  80.2 5.3 %collective-permute-start.43 = (bf16[2,16,2048]{2,1,0:T(8,128)(2,1)S(1)}, bf16[2,16,2048]{2,1,0:T(8,128)(2,1)S(1)}, u32[]{:S(2)}, u32[]{:S(2)}) collective-permute-start(bf16[2,16,2048]{2,1,0:T(8,128)(2,1)S(1)} %collective-permute-done.41.refs_1_), channel_id=1, source_target_pairs={{0,3},{1,0},{2,1},{3,2},{4,7},{5,4},{6,5},{7,6},{8,11},{9,8},{10,9... | collective-permute-start | bytes 393224 | tf_op jit(solution)/shard_map/cond/branch_2_fun/ppermute | solution.py:248
